TPU v7x, 128 devices: a whole 4x4x4 slice. The times are simulated.
128 devices in a mesh: dp: 32 (over y, x_hi, z), outer: 4 (over x_lo, core).
Axes of the slice: x: 4 (x_hi: 2, x_lo: 2; x = x_hi * 2 + x_lo), y: 4, z: 4, core: 2. Of those that a mesh axis runs over, the one named last changes fastest.
Arguments:
- gradients: bfloat16 [128, 1048576], P(('dp', 'outer')), may hold values from -1 to 0.9921875, as said below
- dither: int32 [128, 1048576], P(('dp', 'outer')), may hold values from 0 to 63
- sign_words: int32 [32768], replicated, may hold values from -2147483648 to 2147483646
- level_values: int32 [16], replicated, may hold values from -32 to 32, as said below
- level_points: float32 [16], replicated, may hold values from -1 to 1, as said below
- params: float32 [1048576], replicated, may hold values from -0.3 to 0.3
- first_moment: float32 [1048576], replicated, may hold values from -0.03 to 0.03
- second_moment: float32 [1048576], replicated, may hold values from 2e-05 to 0.01
Outputs:
- new_params: float32 [1048576], replicated
- new_first: float32 [1048576], replicated
- new_second: float32 [1048576], replicated
- update: float32 [1048576], replicated
Inputs may be any that keep to these rules, and one draw needn't show every extreme that they name: `gradients`: every entry is a whole multiple of 1/128. Strictly increasing and antisymmetric (level_values[15 - i] = -level_values[i]); the largest is exactly 32. Strictly increasing and antisymmetric (level_points[15 - i] = -level_points[i]); the largest is exactly 1.
All inputs are finite; a program needn't handle non-finite values.
Results may differ from a plain program's by a relative error of at most 0.0003.
Values sent between devices are 32-bit elements; how exact they have to be, the bound alone decides.
A program may use at most 128 MiB of HBM per device.

v0:
```python
import jax
import jax.numpy as jnp
from jax import lax
from jax.sharding import PartitionSpec as P

HB = 256


beta_first = 0.9
beta_second = 0.95
bias_first = 1.0 - 0.9**50
bias_second = 1.0 - 0.95**50
epsilon = 1e-08
step_rate = 0.01


def hadamard(length):
    indices = jnp.arange(length, dtype=jnp.int32)
    common = indices[:, None] & indices[None, :]
    parity = jnp.zeros((length, length), jnp.int32)
    for bit_pos in range(length.bit_length() - 1):
        parity = parity ^ common >> bit_pos & 1
    return 1 - 2 * parity


def sign_table(sign_words):
    bit_idx = jnp.arange(32, dtype=jnp.int32)
    sign_bits = sign_words[:, None] >> bit_idx[None, :] & 1
    return (1 - 2 * sign_bits).reshape(-1)


def rotate(grad_row, sign_vals, hadamard_bf):
    length = hadamard_bf.shape[0]
    scaled = (grad_row.astype(jnp.float32) * 128.0 * sign_vals.astype(jnp.float32)).astype(
        jnp.bfloat16
    )
    rotated = jnp.dot(scaled.reshape(-1, length), hadamard_bf, preferred_element_type=jnp.float32)
    return rotated.astype(jnp.int32)


def quantize(coeffs, peak_vals, level_values, level_points, dither):
    last_idx = level_values.shape[0] - 1
    target = coeffs * level_values[last_idx]
    peak_col = peak_vals[:, None]
    lower = jnp.zeros(target.shape, jnp.int32) + level_values[0]
    upper = jnp.zeros(target.shape, jnp.int32) + level_values[1]
    lower_point = jnp.zeros(target.shape, jnp.float32) + level_points[0]
    upper_point = jnp.zeros(target.shape, jnp.float32) + level_points[1]
    for level_idx in range(1, last_idx):
        passed = target >= peak_col * level_values[level_idx]
        lower = jnp.where(passed, level_values[level_idx], lower)
        upper = jnp.where(passed, level_values[level_idx + 1], upper)
        lower_point = jnp.where(passed, level_points[level_idx], lower_point)
        upper_point = jnp.where(passed, level_points[level_idx + 1], upper_point)
    rounds_up = 64 * (target - peak_col * lower) > dither * peak_col * (upper - lower)
    return jnp.where(rounds_up, upper_point, lower_point)


def decode_adam(
    totals, peak_vals, sign_vals, hadamard_mat, params, first_moment, second_moment, rank_count
):
    length = totals.shape[1]
    restored = jnp.dot(totals, hadamard_mat.astype(jnp.float32), precision=lax.Precision.HIGHEST)
    factor = peak_vals.astype(jnp.float32) / float(128 * length * rank_count)
    mean_grad = (restored * factor[:, None]).reshape(-1) * sign_vals.astype(jnp.float32)
    new_first = beta_first * first_moment + (1.0 - beta_first) * mean_grad
    new_second = beta_second * second_moment + (1.0 - beta_second) * mean_grad * mean_grad
    update = new_first / bias_first / (jnp.sqrt(new_second / bias_second) + epsilon)
    new_params = params - step_rate * update
    return (new_params, new_first, new_second, update)


def body(
    gradients, dither, sign_words, level_values, level_points, params, first_moment, second_moment
):
    length = HB
    rank_count = lax.axis_size("dp") * lax.axis_size("outer")
    hadamard_mat = hadamard(length)
    sign_vals = sign_table(sign_words)
    coeffs = rotate(gradients[0], sign_vals, hadamard_mat.astype(jnp.bfloat16))
    peak_vals = lax.pmax(jnp.max(jnp.abs(coeffs), axis=1), ("dp", "outer"))
    code_vals = quantize(
        coeffs, peak_vals, level_values, level_points, dither[0].reshape(-1, length)
    )
    owned_sums = lax.psum_scatter(code_vals, "dp", scatter_dimension=0, tiled=True)
    owned_sums = lax.psum(owned_sums, "outer")
    all_sums = lax.all_gather(owned_sums, "dp", axis=0, tiled=True)
    new_params, new_first, new_second, update = decode_adam(
        all_sums,
        peak_vals,
        sign_vals,
        hadamard_mat,
        params,
        first_moment,
        second_moment,
        rank_count,
    )
    return (new_params, new_first, new_second, update)


def solution(mesh):
    placed = (P(("dp", "outer"), None), P(("dp", "outer"), None), P(), P(), P(), P(), P(), P())
    return jax.shard_map(
        body, mesh=mesh, in_specs=placed, out_specs=(P(), P(), P(), P()), check_vma=False
    )
```

profile of v0, /device:TPU:1, one launch (start us, length us, event | category | flops | bytes accessed | tf_op | source)
XLA Modules:
  0.0 568.8 jit_solution(5495611669287808830)
XLA Ops:
  7.3 2.0 fusion.24
  9.3 1.9 fusion.25
  11.2 2.1 shift_right_arithmetic.88
  13.4 0.6 copy.14
  13.9 2.5 shift_right_arithmetic.89
  16.4 5.6 copy.15
  22.5 34.2 %reduce.7 = s32[1048576]{0:T(1024)} reduce(s32[1,1048576]{1,0:T(1,128)} %param.9, s32[]{:T(128)} %broadcast.93), dimensions={0}, to_apply=%param.9.reduce_sub_computation.3 | reduce | bytes 8388612 | tf_op args[1]
  56.7 5.2 reshape_squeeze.3
  61.9 5.6 copy.16
  67.5 46.3 %multiply_reduce_fusion = f32[1048576]{0:T(1024)} fusion(bf16[1,1048576]{1,0:T(2,128)(2,1)} %param.8), kind=kLoop, calls=%fused_computation.12 | loop fusion | flops 2097152 | bytes 6291456 | tf_op jit(solution)/shard_map/mul | solution.py:34
  113.8 5.2 mul.207
  119.0 7.7 %abs_reduce_fusion = (s32[4096]{0:T(1024)S(1)}, s32[4096,256]{0,1:T(8,128)}) fusion(f32[4096,256]{1,0:T(8,128)} %mul.207, s32[4096,256]{1,0:T(8,128)} %copy.15, s32[256]{0:T(256)S(1)} %shift_right_arithmetic.92), kind=kOutput, calls=%fused_computation.10 | convolution fusion | flops 549122048 | bytes 12600320 | tf_op jit(solution)/shard_map/dot_general | solution.py:37
  126.7 68.8 %pmax.7 = s32[4096]{0:T(1024)S(1)} all-reduce(s32[4096]{0:T(1024)S(1)} %get-tuple-element.54), channel_id=1, replica_groups=mesh['dp'=32,'outer'=4] {'dp','outer'}, use_global_device_ids=true, to_apply=%region_1.0 | all-reduce | flops 4096 | bytes 32768 | tf_op jit(solution)/shard_map/pmax | solution.py:81
  195.5 8.8 %broadcast_multiply_fusion.13 = (s32[4096]{0:T(1024)S(1)}, s32[4096]{0:T(1024)S(1)}, s32[4096]{0:T(1024)S(1)}, s32[4096]{0:T(1024)S(1)}, s32[4096]{0:T(1024)S(1)...) fusion(s32[4096]{0:T(1024)S(1)} %pmax.7, ...), kind=kLoop, calls=%fused_computation.34 | loop fusion | flops 57344 | bytes 245816 | tf_op jit(solution)/shard_map/mul | solution.py:50
  204.4 33.1 %select_select_fusion = f32[4096,256]{0,1:T(8,128)} fusion(s32[4096,256]{0,1:T(8,128)} %copy.16, s32[4096,256]{0,1:T(8,128)} %get-tuple-element.55, f32[]{:T(128)} %bitcast.32, f32[]{:T(128)} %bitcast.31, f32[]{:T(128)} %bitcast.30, f32[]{:T(128)} %bitcast.29, f32[]{:T(128)} %bitcast.28, f32[]{:T(128)} %bitcast.27, f32[]{:T(128)} %bitcast.26, f32[]{:T(128)} %bitcast.25, ...), kind=kLoop, calls=%fused_computation.8 | loop fusion | flops 82837504 | bytes 12828800 | tf_op jit(solution)/shard_map/jit(_where)/select_n | solution.py:56
  237.5 165.4 %reduce-scatter.2.cloned.1.call-done = f32[128,256]{0,1:T(8,128)} async-done(((f32[4096,256]{0,1:T(8,128)}), f32[128,256]{0,1:T(8,128)}) %reduce-scatter.2.cloned.1.call-update) | async-done | bytes 131088 | tf_op jit(solution)/shard_map/reduce_scatter | solution.py:85
  403.0 56.4 %all-reduce.2.cloned.1.call-done = f32[128,256]{0,1:T(8,128)} async-done(((f32[128,256]{0,1:T(8,128)}), f32[128,256]{0,1:T(8,128)}) %all-reduce.2.cloned.1.call-update) | async-done | bytes 131088 | tf_op jit(solution)/shard_map/psum | solution.py:86
  459.5 15.6 %subtract_convert_fusion = f32[32768,32]{1,0:T(8,128)} fusion(s32[32768]{0:T(1024)S(1)} %copy-done.2), kind=kLoop, calls=%fused_computation | loop fusion | flops 5242880 | bytes 4325376 | tf_op jit(solution)/shard_map/convert_element_type | solution.py:34
  475.1 12.0 %reshape.64 = f32[1048576]{0:T(1024)} reshape(f32[32768,32]{1,0:T(8,128)} %subtract_convert_fusion) | data formatting | bytes 8388608 | tf_op jit(solution)/shard_map/convert_element_type | solution.py:34
  487.1 53.1 %all-gather.2.cloned.1.call-done = f32[4096,256]{0,1:T(8,128)} async-done(((f32[128,256]{0,1:T(8,128)}), f32[4096,256]{0,1:T(8,128)}) %all-gather.2.cloned.1.call-update) | async-done | bytes 4194320 | tf_op jit(solution)/shard_map/all_gather | solution.py:87
  540.1 9.6 %fusion.1 = f32[512,2,8,128]{3,2,1,0:T(8,128)S(1)} fusion(f32[4096,256]{0,1:T(8,128)} %all-gather.2.cloned.1.call-done, f32[4096]{0:T(1024)S(1)} %convert_multiply_fusion), kind=kOutput, calls=%fused_computation.13 | convolution fusion | flops 3224043520 | bytes 8404992 | tf_op jit(solution)/shard_map/dot_general | solution.py:63
  549.7 2.2 copy.17
  551.9 1.3 copy-done.1
  553.2 9.1 %multiply_subtract_fusion = (f32[1048576]{0:T(1024)}, f32[1048576]{0:T(1024)}, f32[1048576]{0:T(1024)}, f32[1048576]{0:T(1024)}) fusion(f32[1048576]{0:T(1024)S(1)} %copy-done.1, f32[1048576]{0:T(1024)S(1)} %bitcast.37, f32[1048576]{0:T(1024)S(1)} %copy-done, f32[1048576]{0:T(1024)} %param.14, f32[1048576]{0:T(1024)} %param.15), kind=kLoop, calls=%fused_computation.5 | loop fusion | flops 14680064 | bytes 37748736 | tf_op jit(solution)/shard_map/sub | solution.py:69
  (15 shorter events, 0.8 us)
Async XLA Ops:
  7.2 395.8 %reduce-scatter.2.cloned.1.call-start = ((), (), s32[]{:S(2)}) async-start(), calls=%async_computation.1 | async-start | bytes 4325376 | tf_op jit(solution)/shard_map/reduce_scatter | solution.py:85
  237.5 222.0 %copy-start.2 = (s32[32768]{0:T(1024)S(1)}, s32[32768]{0:T(1024)}, u32[]{:S(2)}) copy-start(s32[32768]{0:T(1024)} %param.10) | copy-start | bytes 393220
  237.5 222.0 %all-reduce.2.cloned.1.call-start = ((), (), s32[]{:S(2)}) async-start(), calls=%async_computation.2 | async-start | bytes 262144 | tf_op jit(solution)/shard_map/psum | solution.py:86
  403.0 137.1 %all-gather.2.cloned.1.call-start = ((), (), s32[]{:S(2)}) async-start(), calls=%async_computation.3 | async-start | bytes 4325376 | tf_op jit(solution)/shard_map/all_gather | solution.py:87
  549.7 2.2 copy-start
  549.7 3.5 copy-start.1
Sparse Core Ops, SparseCore 0:
  237.6 165.2 reduce-scatter.1
  405.4 53.9 all-reduce.1
  462.6 77.4 all-gather.1
where the time goes:
time: 570 us; the launch traced here: 569 us
  waiting for transfers between devices  275 us (48%)
  other arithmetic  147 us (26%)
  blocking collectives  68.8 us (12%)
  local copies, waits for them, and re-layouts  46.7 us (8%)
  matrix products  17.3 us (3%)
  between operations  13.8 us (2%)
    reduce_scatter x1, waiting for transfers between devices, body(): lax.psum_scatter(code_vals, 'dp', scatter_dimension=0, tiled=True)  165 us
    pmax x1, blocking collectives, body(): peak_vals = lax.pmax(jnp.max(jnp.abs(coeffs), axis=1), ('dp', 'outer'))  68.8 us
    psum x1, waiting for transfers between devices, body(): owned_sums = lax.psum(owned_sums, 'outer')  56.4 us
    all_gather x1, waiting for transfers between devices, body(): all_sums = lax.all_gather(owned_sums, 'dp', axis=0, tiled=True)  53.1 us
    mul x1, other arithmetic, rotate(): grad_row.astype(jnp.float32) * 128.0 * sign_vals.astype(jnp.float32)  46.3 us
    unnamed x1, other arithmetic  34.2 us
    select_n x1, other arithmetic, quantize(): return jnp.where(rounds_up, upper_point, lower_point)  33.1 us
    convert_element_type x1, other arithmetic, rotate(): sign_vals.astype(jnp.float32)  15.6 us
  transfers between devices with their start and end apart: 3, of which 3 were waited for; matrix products, arithmetic and copies ran while one was open for 5% of the time, Pallas kernels for 0%

commit v1 on v0

v1 whole, which is shorter than its diff:
```python
import jax
import jax.numpy as jnp
from jax import lax
from jax.experimental import pallas as pl
from jax.experimental.pallas import tpu as pltpu
from jax.sharding import PartitionSpec as P

MESH = pl.DeviceIdType.MESH
LANES = 128
UNIT = 8
ROWS = 8192
HALF_ROWS = ROWS // 2
CHUNK = 1024
RING = 4
SEGMENTS = ((0, 192), (192, 192), (384, 128))
ORDERS = (("x", "y", "z"), ("y", "z", "x"), ("z", "x", "y"))

beta_first = 0.9
beta_second = 0.95
bias_first = 1.0 - 0.9**50
bias_second = 1.0 - 0.95**50
epsilon = 1e-08
step_rate = 0.01


def rows_of(start, count):
    return pl.ds(pl.multiple_of(start * UNIT, UNIT), count * UNIT)


def take(table, idx):
    return jnp.take_along_axis(table, idx, axis=1, mode="promise_in_bounds")


def hadamard_128(length):
    common = lax.broadcasted_iota(jnp.int32, (length, length), 0) & lax.broadcasted_iota(
        jnp.int32, (length, length), 1
    )
    for shift in (4, 2, 1):
        common = common ^ (common >> shift)
    return jnp.where((common & 1) == 1, -128.0, 128.0).astype(jnp.float32)


class Place:
    def __init__(self):
        dp, outer = lax.axis_index("dp"), lax.axis_index("outer")
        self.at = {
            "y": lax.div(dp, 8),
            "x": lax.rem(lax.div(dp, 4), 2) * 2 + lax.div(outer, 2),
            "z": lax.rem(dp, 4),
            "core": lax.rem(outer, 2),
        }

    def near(self, axis, delta):
        at = dict(self.at)
        size = 2 if axis == "core" else RING
        at[axis] = lax.rem(at[axis] + (delta % size), size)
        dp = at["y"] * 8 + lax.div(at["x"], 2) * 4 + at["z"]
        return {"dp": dp, "outer": lax.rem(at["x"], 2) * 2 + at["core"]}


class Copies:
    def __init__(self, send, recv):
        self.send, self.recv, self.used, self.all = send, recv, 0, []

    def start(self, src, dst, to):
        copy = pltpu.make_async_remote_copy(
            src_ref=src,
            dst_ref=dst,
            send_sem=self.send.at[self.used],
            recv_sem=self.recv.at[self.used],
            device_id=to,
            device_id_type=MESH,
        )
        self.used += 1
        self.all.append(copy)
        copy.start()
        return copy

    def finish(self):
        for copy in self.all:
            copy.wait_send()


COPIES = 10 + 3 + 54 + 54 + 12


def layout():
    places, used = {}, 0
    for stage in range(3):
        for seg, (_, size) in enumerate(SEGMENTS):
            quarter = size // RING ** (stage + 1)
            low = quarter // 2
            for name, count in (("tl", low), ("th", quarter - low), ("fa", quarter), ("fb", quarter)):
                places[stage, seg, name] = (used, count)
                used += count
    return places, used


def add_into(dst, start, sources, count):
    step = 8 if count % 8 == 0 and count > 12 else count

    def body(i, carry):
        here = rows_of(start + i * step, step)
        value = dst[here, :]
        for ref, first in sources:
            value = value + ref[rows_of(first + i * step, step), :]
        dst[here, :] = value
        return carry

    if step == count:
        body(0, 0)
    else:
        lax.fori_loop(0, count // step, body, 0)


def reduce_kernel(
    grad_hbm, dither_hbm, words, level_values, level_points, out,
    grad_v, dither_v, signed, coef_even, coef_odd, codes, peaks, scaled, recip, peak_in,
    sibling_in, landing, owned, send_sems, recv_sems, grad_sems, dither_sem,
):
    here = Place()
    copies = Copies(send_sems, recv_sems)
    chunks = ROWS // CHUNK
    span = CHUNK * LANES
    loads = [
        pltpu.make_async_copy(
            grad_hbm.at[:, pl.ds(i * span, span)], grad_v.at[:, pl.ds(i * span, span)], grad_sems.at[i]
        )
        for i in range(chunks)
    ]
    for load in loads:
        load.start()
    dither_load = pltpu.make_async_copy(dither_hbm, dither_v, dither_sem)
    dither_load.start()

    barrier = pltpu.get_barrier_semaphore()
    partners = [here.near("core", 1)]
    for axis in ("x", "y", "z"):
        partners += [here.near(axis, delta) for delta in (1, 2, 3)]
    for partner in partners:
        pl.semaphore_signal(barrier, inc=1, device_id=partner, device_id_type=MESH)

    lane = lax.broadcasted_iota(jnp.int32, (UNIT, LANES), 1)
    sub = lax.broadcasted_iota(jnp.int32, (UNIT, LANES), 0)
    word_lane = sub * 4 + (lane >> 5)
    word_shift = 31 - (lane & 31)
    had = hadamard_128(2 * LANES)
    had_bf = had.astype(jnp.bfloat16)

    for i in range(chunks):
        loads[i].wait()

        def sign_rows(r, carry, i=i):
            word_row = i * (CHUNK // 32) + r
            wide = jnp.broadcast_to(words[pl.ds(word_row, 1), :], (UNIT, LANES))
            for k in range(4):
                word = take(wide, word_lane + 32 * k)
                first = pl.multiple_of(word_row * 4096 + k * 1024, 1024)
                grad = grad_v[:, pl.ds(first, 1024)].astype(jnp.float32).reshape(UNIT, LANES)
                signed[rows_of(r * 4 + k, 1), :] = jnp.where((word << word_shift) < 0, -grad, grad)
            return carry

        lax.fori_loop(0, CHUNK // 32, sign_rows, 0, unroll=4)
        even = signed[pl.ds(0, CHUNK // 2, stride=2), :]
        odd = signed[pl.ds(1, CHUNK // 2, stride=2), :]
        both = jnp.concatenate([even, odd], axis=1).astype(jnp.bfloat16)
        coeffs = jnp.dot(both, had_bf, preferred_element_type=jnp.float32)
        at = pl.ds(i * (CHUNK // 2), CHUNK // 2)
        coef_even[at, :] = coeffs[:, :LANES]
        coef_odd[at, :] = coeffs[:, LANES:]
        turned = lax.dot_general(
            had_bf, both, (((1,), (1,)), ((), ())), preferred_element_type=jnp.float32
        )
        top = jnp.max(jnp.abs(turned), axis=0, keepdims=True)
        for j in range(CHUNK // 256):
            peaks[pl.ds(i * (CHUNK // 256) + j, 1), :] = top[:, j * LANES : (j + 1) * LANES]

    pl.semaphore_wait(barrier, len(partners))
    used = 0
    for axis, deltas in (("core", (1,)), ("x", (1, 2, 3)), ("y", (1, 2, 3)), ("z", (1, 2, 3))):
        sent = []
        for delta in deltas:
            sent.append(copies.start(peaks, peak_in.at[used], here.near(axis, delta)))
            used += 1
        for copy in sent:
            copy.wait_recv()
            copy.wait_send()
        best = peaks[...]
        for slot in range(used - len(deltas), used):
            best = jnp.maximum(best, peak_in[slot])
        peaks[...] = best
    top = peaks[...]
    scaled[...] = top * (1.0 / 32.0)
    recip[...] = 32.0 / jnp.maximum(top, 1.0)

    cell = (lane & 63) - 32
    low = jnp.full((UNIT, LANES), level_values[0], jnp.int32)
    high = jnp.full((UNIT, LANES), level_values[1], jnp.int32)
    low_point = jnp.full((UNIT, LANES), level_points[0], jnp.float32)
    high_point = jnp.full((UNIT, LANES), level_points[1], jnp.float32)
    for j in range(1, 15):
        passed = cell >= level_values[j]
        low = jnp.where(passed, level_values[j], low)
        high = jnp.where(passed, level_values[j + 1], high)
        low_point = jnp.where(passed, level_points[j], low_point)
        high_point = jnp.where(passed, level_points[j + 1], high_point)
    gap_table = low.astype(jnp.float32) + (high - low).astype(jnp.float32) * (1.0 / 64.0)
    point_table = jnp.where(lane < 64, low_point, high_point)

    dither_load.wait()

    def quantize_rows(peak_row, add):
        scaled_row = jnp.broadcast_to(scaled[pl.ds(peak_row, 1), :], (UNIT, LANES))
        recip_row = jnp.broadcast_to(recip[pl.ds(peak_row, 1), :], (UNIT, LANES))
        for m in range(16):
            idx = sub + 8 * m
            peak32 = take(scaled_row, idx)
            ratio = take(recip_row, idx)
            peak_high = jnp.floor(peak32 * 0.125) * 8.0
            peak_low = peak32 - peak_high
            for parity, coef in ((0, coef_even), (1, coef_odd)):
                value = coef[rows_of(peak_row * 16 + m, 1), :]
                at = pl.ds(peak_row * 256 + (16 * m + parity), UNIT, stride=2)
                offset = dither_v[at, :].astype(jnp.float32)
                place = jnp.minimum((value * ratio + 32.0).astype(jnp.int32), 63)
                packed = take(gap_table, place)
                whole = jnp.floor(packed)
                bound = whole + offset * (packed - whole)
                up = (value - peak_high * bound) > peak_low * bound
                code = take(point_table, jnp.where(up, place + 64, place))
                if add:
                    near = pl.ds(lax.rem(peak_row, 16) * 256 + (16 * m + parity), UNIT, stride=2)
                    code = code + sibling_in[near, :]
                codes[at, :] = code

    core = here.at["core"]
    mine, theirs = core * 512, (1 - core) * 512
    sibling = here.near("core", 1)
    halves = []
    for first, size in SEGMENTS:

        def other(r, carry, first=first):
            quantize_rows((theirs + first) // 32 + r, False)
            return carry

        lax.fori_loop(0, size // 32, other, 0)
        halves.append(
            copies.start(codes.at[rows_of(theirs + first, size)], sibling_in.at[rows_of(first, size)], sibling)
        )

    places, _ = layout()

    def land(stage, seg, name, skip=0, count=None):
        first, size = places[stage, seg, name]
        return landing.at[rows_of(first + skip, size if count is None else count)]

    base = [mine + first for first, _ in SEGMENTS]
    bases = [[None] * 3 for _ in SEGMENTS]
    pending = {}

    def cut(stage, seg):
        quarter = SEGMENTS[seg][1] // RING ** (stage + 1)
        low_part = quarter // 2
        axis = ORDERS[seg][stage]
        p = here.at[axis]
        start = bases[seg][stage]
        part = [start + lax.rem(p + d, RING) * quarter for d in range(RING)]
        return quarter, low_part, part, here.near(axis, 1), here.near(axis, 3)

    def scatter_first(stage, seg):
        bases[seg][stage] = base[seg]
        quarter, low_part, part, right, left = cut(stage, seg)
        high_part = quarter - low_part
        pending[stage, seg] = [
            copies.start(codes.at[rows_of(part[2], low_part)], land(stage, seg, "tl"), right),
            copies.start(codes.at[rows_of(part[2] + low_part, high_part)], land(stage, seg, "th"), left),
            copies.start(
                codes.at[rows_of(part[1] + low_part, high_part)],
                land(stage, seg, "fa", low_part, high_part),
                right,
            ),
            copies.start(codes.at[rows_of(part[3], low_part)], land(stage, seg, "fb", 0, low_part), left),
        ]

    def scatter_second(stage, seg):
        quarter, low_part, part, right, left = cut(stage, seg)
        high_part = quarter - low_part
        waits = pending[stage, seg]
        waits[0].wait_recv()
        add_into(codes, part[1], [(landing, places[stage, seg, "tl"][0])], low_part)
        waits.append(
            copies.start(codes.at[rows_of(part[1], low_part)], land(stage, seg, "fa", 0, low_part), right)
        )
        waits[1].wait_recv()
        add_into(codes, part[3] + low_part, [(landing, places[stage, seg, "th"][0])], high_part)
        waits.append(
            copies.start(
                codes.at[rows_of(part[3] + low_part, high_part)],
                land(stage, seg, "fb", low_part, high_part),
                left,
            )
        )

    def scatter_last(stage, seg):
        quarter, _, part, _, _ = cut(stage, seg)
        for copy in pending[stage, seg][2:]:
            copy.wait_recv()
        add_into(
            codes,
            part[0],
            [(landing, places[stage, seg, "fa"][0]), (landing, places[stage, seg, "fb"][0])],
            quarter,
        )
        base[seg] = part[0]

    for seg, (first, size) in enumerate(SEGMENTS):
        halves[seg].wait_recv()

        def own(r, carry, first=first):
            quantize_rows((mine + first) // 32 + r, True)
            return carry

        lax.fori_loop(0, size // 32, own, 0)
        scatter_first(0, seg)

    for stage in range(3):
        for seg in range(3):
            scatter_second(stage, seg)
        for seg in range(3):
            scatter_last(stage, seg)
            if stage < 2:
                scatter_first(stage + 1, seg)

    units = [base[seg] + i for seg, (_, size) in enumerate(SEGMENTS) for i in range(size // 64)]
    for i, unit in enumerate(units):
        owned[pl.ds(i * UNIT, UNIT), :] = codes[rows_of(unit, 1), :]
    count = len(units) * UNIT // 2
    both = jnp.concatenate(
        [owned[pl.ds(0, count, stride=2), :], owned[pl.ds(1, count, stride=2), :]], axis=1
    )
    back = jnp.dot(both, had, precision=lax.Precision.HIGHEST, preferred_element_type=jnp.float32)
    owned[pl.ds(0, count, stride=2), :] = back[:, :LANES]
    owned[pl.ds(1, count, stride=2), :] = back[:, LANES:]
    for i, unit in enumerate(units):
        wide = jnp.broadcast_to(words[pl.ds(lax.div(unit, 4), 1), :], (UNIT, LANES))
        word = take(wide, word_lane + 32 * lax.rem(unit, 4))
        wide = jnp.broadcast_to(scaled[pl.ds(lax.div(unit, 32), 1), :], (UNIT, LANES))
        factor = take(wide, 4 * lax.rem(unit, 32) + (sub >> 1)) * (1.0 / 2.0**24)
        grad = owned[pl.ds(i * UNIT, UNIT), :] * factor
        out[rows_of(unit, 1), :] = jnp.where((word << word_shift) < 0, -grad, grad)

    def send(start, size, to):
        at = rows_of(start, size)
        return copies.start(out.at[at], out.at[at], to)

    last = []

    def gather_first(stage, seg):
        quarter, low_part, part, right, left = cut(stage, seg)
        high_part = quarter - low_part
        pending[stage, seg] = [
            send(part[0], low_part, right),
            send(part[0] + low_part, high_part, left),
            send(part[0] + low_part, high_part, right),
            send(part[0], low_part, left),
        ]
        if stage == 0:
            last.append(send(part[0], quarter, sibling))

    def gather_second(stage, seg):
        quarter, low_part, part, right, left = cut(stage, seg)
        high_part = quarter - low_part
        waits = pending[stage, seg]
        waits[0].wait_recv()
        waits.append(send(part[3], low_part, right))
        waits[1].wait_recv()
        waits.append(send(part[1] + low_part, high_part, left))
        waits[2].wait_recv()
        waits[3].wait_recv()
        if stage == 0:
            last.append(send(part[3], quarter, sibling))
            last.append(send(part[1], quarter, sibling))

    def gather_last(stage, seg):
        quarter, _, part, _, _ = cut(stage, seg)
        for copy in pending[stage, seg][4:]:
            copy.wait_recv()
        if stage == 0:
            last.append(send(part[2], quarter, sibling))

    for stage in (2, 1, 0):
        for seg in range(3):
            gather_first(stage, seg)
        for seg in range(3):
            gather_second(stage, seg)
        for seg in range(3):
            gather_last(stage, seg)
    for copy in last:
        copy.wait_recv()
    for copy in copies.all[10:]:
        copy.wait_send()


def mean_gradient(gradients, dither, sign_words, level_values, level_points):
    units = layout()[1]
    whole = pltpu.VMEM((ROWS, LANES), jnp.float32)
    half = pltpu.VMEM((HALF_ROWS, LANES), jnp.float32)
    peak = pltpu.VMEM((ROWS // 256, LANES), jnp.float32)
    anywhere = pl.BlockSpec(memory_space=pl.ANY)
    vmem = pl.BlockSpec(memory_space=pltpu.VMEM)
    smem = pl.BlockSpec(memory_space=pltpu.SMEM)
    return pl.pallas_call(
        reduce_kernel,
        out_shape=jax.ShapeDtypeStruct((ROWS, LANES), jnp.float32),
        in_specs=[anywhere, anywhere, vmem, smem, smem],
        out_specs=vmem,
        scratch_shapes=[
            pltpu.VMEM((1, ROWS * LANES), jnp.bfloat16),
            pltpu.VMEM((ROWS, LANES), jnp.int32),
            pltpu.VMEM((CHUNK, LANES), jnp.float32),
            half,
            half,
            whole,
            peak,
            peak,
            peak,
            pltpu.VMEM((10, ROWS // 256, LANES), jnp.float32),
            half,
            pltpu.VMEM((units * UNIT, LANES), jnp.float32),
            pltpu.VMEM((64, LANES), jnp.float32),
            pltpu.SemaphoreType.DMA((COPIES,)),
            pltpu.SemaphoreType.DMA((COPIES,)),
            pltpu.SemaphoreType.DMA((ROWS // CHUNK,)),
            pltpu.SemaphoreType.DMA,
        ],
        compiler_params=pltpu.CompilerParams(
            collective_id=0, has_side_effects=True, vmem_limit_bytes=44 * 2**20
        ),
        cost_estimate=pl.CostEstimate(flops=2**31, bytes_accessed=12 * 2**20, transcendentals=0),
    )(
        gradients,
        dither.reshape(ROWS, LANES),
        sign_words.reshape(-1, LANES),
        level_values,
        level_points,
    )


def body(
    gradients, dither, sign_words, level_values, level_points, params, first_moment, second_moment
):
    mean_grad = mean_gradient(gradients, dither, sign_words, level_values, level_points).reshape(-1)
    new_first = beta_first * first_moment + (1.0 - beta_first) * mean_grad
    new_second = beta_second * second_moment + (1.0 - beta_second) * mean_grad * mean_grad
    update = new_first / bias_first / (jnp.sqrt(new_second / bias_second) + epsilon)
    new_params = params - step_rate * update
    return (new_params, new_first, new_second, update)


def solution(mesh):
    placed = (P(("dp", "outer"), None), P(("dp", "outer"), None), P(), P(), P(), P(), P(), P())
    return jax.shard_map(
        body, mesh=mesh, in_specs=placed, out_specs=(P(), P(), P(), P()), check_vma=False
    )
```

time: 570 us -> 101 us (0.18)
  waiting for transfers between devices: 275 us -> 0 us
  other arithmetic: 147 us -> 8.29 us
  Pallas kernels: 0 us -> 87.7 us
  blocking collectives: 68.8 us -> 0 us
  local copies, waits for them, and re-layouts: 46.7 us -> 4.4 us
  matrix products: 17.3 us -> 0 us
  between operations: 13.8 us -> 0.67 us
    reduce_scatter x1 -> x0, waiting for transfers between devices: 165 us -> none  [body(): lax.psum_scatter(code_vals, 'dp', scatter_dimension=0, tiled=True)]
    pallas_call x0 -> x1, Pallas kernels: none -> 87.7 us  [mean_gradient(): pl.pallas_call(reduce_kernel, out_shape=jax.ShapeDtypeStruct((ROWS, LANES...]
    pmax x1 -> x0, blocking collectives: 68.8 us -> none  [body(): peak_vals = lax.pmax(jnp.max(jnp.abs(coeffs), axis=1), ('dp', 'outer'))]
    psum x1 -> x0, waiting for transfers between devices: 56.4 us -> none  [body(): owned_sums = lax.psum(owned_sums, 'outer')]
    mul x2 -> x0, other arithmetic: 55.2 us -> none  [the longest x1 46.3 us: rotate(): grad_row.astype(jnp.float32) * 128.0 * sign_vals.astype(jnp.float32)]
    all_gather x1 -> x0, waiting for transfers between devices: 53.1 us -> none  [body(): all_sums = lax.all_gather(owned_sums, 'dp', axis=0, tiled=True)]
    unnamed x1 -> x0, other arithmetic: 34.2 us -> none
    select_n x1 -> x0, other arithmetic: 33.1 us -> none  [quantize(): return jnp.where(rounds_up, upper_point, lower_point)]
  transfers between devices with their start and end apart: 3 -> 0, of which waited for: 3 -> 0; matrix products, arithmetic and copies ran while one was open for 5% -> 0% of each run, Pallas kernels for 0% -> 0%
where the time goes in v1:
time: 101 us
  Pallas kernels  87.7 us (87%)
  other arithmetic  8.29 us (8%)
  local copies, waits for them, and re-layouts  4.4 us (4%)
    pallas_call x1, Pallas kernels, mean_gradient(): pl.pallas_call(reduce_kernel, out_shape=jax.ShapeDtypeStruct((ROWS, LANES...  87.7 us
    sub x1, other arithmetic, body(): new_params = params - step_rate * update  8.29 us
    unnamed x12, local copies, waits for them, and re-layouts  4.4 us

profile of v1, /device:TPU:1, one launch (start us, length us, event | category | flops | bytes accessed | tf_op | source)
XLA Modules:
  0.0 101.1 jit_solution(8149136457399663946)
XLA Ops:
  0.6 0.0 copy-start
  0.6 2.2 %copy-done = bf16[1,1048576]{1,0:T(2,128)(2,1)S(1)} copy-done((bf16[1,1048576]{1,0:T(2,128)(2,1)S(1)}, bf16[1,1048576]{1,0:T(2,128)(2,1)}, u32[]{:S(2)}) %copy-start) | copy-done | bytes 2097176
  2.8 0.0 copy-start.1
  2.8 0.9 copy-done.1
  3.7 0.0 copy-start.2
  3.7 0.7 copy-done.2
  4.4 0.0 copy-start.3
  4.4 0.7 copy-done.3
  5.0 0.0 copy-start.4
  5.0 0.0 copy-start.5
  5.0 87.7 %shard_map.111 = f32[8192,128]{1,0:T(8,128)S(1)} custom-call(bf16[1,1048576]{1,0:T(2,128)(2,1)S(1)} %copy-done, s32[8192,128]{1,0:T(8,128)} %bitcast.10, s32[256,128]{1,0:T(8,128)S(1)} %bitcast.9, s32[16]{0:T(128)S(1)} %copy-done.2, f32[16]{0:T(128)S(1)} %copy-done.3), custom_call_target="tpu_custom_call" | custom-call | flops 2147483648 | bytes 12582912 | tf_op jit(solution)/shard_map/pallas_call | solution.py:412
  92.8 0.0 copy-done.4
  92.8 0.0 copy-done.5
  92.8 8.3 %multiply_subtract_fusion = (f32[1048576]{0:T(1024)}, f32[1048576]{0:T(1024)}, f32[1048576]{0:T(1024)}, f32[1048576]{0:T(1024)}) fusion(f32[1048576]{0:T(1024)S(1)} %copy-done.4, f32[8192,128]{1,0:T(8,128)S(1)} %shard_map.111, f32[1048576]{0:T(1024)S(1)} %copy-done.5, f32[1048576]{0:T(1024)} %param.15), kind=kLoop, calls=%fused_computation.4 | loop fusion | flops 13631488 | bytes 33554432 | tf_op jit(solution)/shard_map/sub | solution.py:456
Async XLA Ops:
  0.6 2.2 %copy-start = (bf16[1,1048576]{1,0:T(2,128)(2,1)S(1)}, bf16[1,1048576]{1,0:T(2,128)(2,1)}, u32[]{:S(2)}) copy-start(bf16[1,1048576]{1,0:T(2,128)(2,1)} %grad_hbm.1) | copy-start | bytes 6291460
  2.8 0.9 copy-start.1
  3.7 0.7 copy-start.2
  4.4 0.7 copy-start.3
  5.0 87.7 %copy-start.4 = (f32[1048576]{0:T(1024)S(1)}, f32[1048576]{0:T(1024)}, u32[]{:S(2)}) copy-start(f32[1048576]{0:T(1024)} %param.13) | copy-start | bytes 12582916
  5.0 87.7 %copy-start.5 = (f32[1048576]{0:T(1024)S(1)}, f32[1048576]{0:T(1024)}, u32[]{:S(2)}) copy-start(f32[1048576]{0:T(1024)} %param.14) | copy-start | bytes 12582916

commit v2 on v1

v2 whole, which is shorter than its diff:
```python
import jax
import jax.numpy as jnp
from jax import lax
from jax.experimental import pallas as pl
from jax.experimental.pallas import tpu as pltpu
from jax.sharding import PartitionSpec as P

MESH = pl.DeviceIdType.MESH
LANES = 128
UNIT = 8
ROWS = 8192
HALF_ROWS = ROWS // 2
CHUNK = 512
RING = 4
SEGMENTS = ((0, 192), (192, 192), (384, 128))
ORDERS = (("x", "y", "z"), ("y", "z", "x"), ("z", "x", "y"))
PLANE = tuple((i, j) for i in (2, 1, 3, 0) for j in (2, 1, 3, 0) if i + j)
GROUPS = (0, 1, 3, 2)
BATCH = 16
PEAK_ROWS = 2

beta_first = 0.9
beta_second = 0.95
bias_first = 1.0 - 0.9**50
bias_second = 1.0 - 0.95**50
epsilon = 1e-08
step_rate = 0.01


def rows_of(start, count):
    return pl.ds(pl.multiple_of(start * UNIT, UNIT), count * UNIT)


def take(table, idx):
    return jnp.take_along_axis(table, idx, axis=1, mode="promise_in_bounds")


def hadamard_128(length):
    common = lax.broadcasted_iota(jnp.int32, (length, length), 0) & lax.broadcasted_iota(
        jnp.int32, (length, length), 1
    )
    for shift in (4, 2, 1):
        common = common ^ (common >> shift)
    return jnp.where((common & 1) == 1, -128.0, 128.0).astype(jnp.float32)


class Place:
    def __init__(self):
        dp, outer = lax.axis_index("dp"), lax.axis_index("outer")
        self.at = {
            "y": lax.div(dp, 8),
            "x": lax.rem(lax.div(dp, 4), 2) * 2 + lax.div(outer, 2),
            "z": lax.rem(dp, 4),
            "core": lax.rem(outer, 2),
        }

    def near(self, *moves):
        at = dict(self.at)
        for axis, delta in moves:
            at[axis] = lax.rem(at[axis] + delta, 2 if axis == "core" else RING)
        dp = at["y"] * 8 + lax.div(at["x"], 2) * 4 + at["z"]
        return {"dp": dp, "outer": lax.rem(at["x"], 2) * 2 + at["core"]}


class Copies:
    def __init__(self, send, recv):
        self.send, self.recv, self.all = send, recv, []

    def start(self, src, dst, to):
        copy = pltpu.make_async_remote_copy(
            src_ref=src,
            dst_ref=dst,
            send_sem=self.send.at[len(self.all)],
            recv_sem=self.recv.at[len(self.all)],
            device_id=to,
            device_id_type=MESH,
        )
        self.all.append(copy)
        copy.start()
        return copy


PEAK_FIRST = tuple((("x", i), ("core", j)) for i in (2, 1, 3, 0) for j in (1, 0) if i + j)
PEAK_SECOND = tuple((("y", i), ("z", j)) for i, j in PLANE)
COPIES = 3 * (7 + 15 + 1 + 6 + 15 + 15 + 4 * 10)


def layout():
    places, used = {}, 0
    for seg, (_, size) in enumerate(SEGMENTS):
        quarter = size // RING
        low = quarter // 2
        for name, count in (
            ("tl", low),
            ("th", quarter - low),
            ("fa", quarter),
            ("fb", quarter),
            ("plane", quarter),
        ):
            places[seg, name] = (used, count)
            used += count
    return places, used


def add_into(dst, start, sources, count):
    step = 8 if count % 8 == 0 and count > 12 else count

    def body(i, carry):
        here = rows_of(start + i * step, step)
        value = dst[here, :]
        for ref, first in sources:
            value = value + ref[rows_of(first + i * step, step), :]
        dst[here, :] = value
        return carry

    if step == count:
        body(0, 0)
    else:
        lax.fori_loop(0, count // step, body, 0)


def reduce_kernel(
    grad_hbm, dither_hbm, words_hbm, values_hbm, points_hbm, out,
    grad_v, dither_v, words, level_values, level_points, signed, coef_even, coef_odd, codes,
    peak_a, peak_b, peak_c, first_in, second_in, high_all, low_all, ratio_all,
    sibling_in, landing, owned, send_sems, recv_sems, grad_sems, load_sems,
):
    here = Place()
    core = here.at["core"]
    copies = Copies(send_sems, recv_sems)
    peaks = (peak_a, peak_b, peak_c)
    sibling = here.near(("core", 1))
    mine, theirs = core * 512, (1 - core) * 512

    small_loads = [
        pltpu.make_async_copy(src, dst, load_sems.at[i])
        for i, (src, dst) in enumerate(
            ((words_hbm, words), (values_hbm, level_values), (points_hbm, level_points), (dither_hbm, dither_v))
        )
    ]
    span = CHUNK * LANES
    small_loads[0].start()
    steps = []
    for seg, (first, size) in enumerate(SEGMENTS):
        for half in (theirs, mine):
            steps += [(seg, half, (half + first) // 64 + i, i) for i in range(size // 64)]
    loads = []
    for i, (_, _, chunk, _) in enumerate(steps):
        at = pl.ds(pl.multiple_of(chunk * span, span), span)
        loads.append(pltpu.make_async_copy(grad_hbm.at[:, at], grad_v.at[:, at], grad_sems.at[i]))
        loads[-1].start()
    for load in small_loads[1:]:
        load.start()

    barrier = pltpu.get_barrier_semaphore()
    partners = [here.near(*moves) for moves in PEAK_FIRST + PEAK_SECOND]
    for a1, a2 in (("z", "x"), ("x", "y")):
        for i in (1, 2, 3):
            for j in (1, 2, 3):
                partners.append(here.near((a1, i), (a2, j)))
    for partner in partners:
        pl.semaphore_signal(barrier, inc=1, device_id=partner, device_id_type=MESH)

    lane = lax.broadcasted_iota(jnp.int32, (UNIT, LANES), 1)
    sub = lax.broadcasted_iota(jnp.int32, (UNIT, LANES), 0)
    word_lane = sub * 4 + (lane >> 5)
    word_shift = 31 - (lane & 31)
    had = hadamard_128(2 * LANES)
    had_bf = had.astype(jnp.bfloat16)
    for ref in peaks:
        ref[...] = jnp.zeros_like(ref)

    def rotate(step):
        seg, half, chunk, i = steps[step]
        loads[step].wait()

        def sign_rows(r, carry):
            word_row = chunk * (CHUNK // 32) + r
            wide = jnp.broadcast_to(words[pl.ds(word_row, 1), :], (UNIT, LANES))
            for k in range(4):
                word = take(wide, word_lane + 32 * k)
                first = pl.multiple_of(word_row * 4096 + k * 1024, 1024)
                grad = grad_v[:, pl.ds(first, 1024)].astype(jnp.float32).reshape(UNIT, LANES)
                signed[rows_of(r * 4 + k, 1), :] = jnp.where((word << word_shift) < 0, -grad, grad)
            return carry

        lax.fori_loop(0, CHUNK // 32, sign_rows, 0, unroll=4)
        even = signed[pl.ds(0, CHUNK // 2, stride=2), :]
        odd = signed[pl.ds(1, CHUNK // 2, stride=2), :]
        both = jnp.concatenate([even, odd], axis=1).astype(jnp.bfloat16)
        coeffs = jnp.dot(both, had_bf, preferred_element_type=jnp.float32)
        at = rows_of(chunk * 32, 32)
        coef_even[at, :] = coeffs[:, :LANES]
        coef_odd[at, :] = coeffs[:, LANES:]
        turned = lax.dot_general(
            had_bf, both, (((1,), (1,)), ((), ())), preferred_element_type=jnp.float32
        )
        top = jnp.max(jnp.abs(turned), axis=0, keepdims=True)
        half_core = lax.div(half, 512)
        for j in range(2):
            row = half_core * (peaks[seg].shape[0] // 2) + (2 * i + j)
            peaks[seg][pl.ds(row, 1), :] = top[:, j * LANES : (j + 1) * LANES]

    def peak_send(seg, partners_of, arrivals):
        return [
            copies.start(peaks[seg], arrivals.at[seg, slot, pl.ds(0, peaks[seg].shape[0])], here.near(*moves))
            for slot, moves in enumerate(partners_of)
        ]

    def peak_take(seg, sent, arrivals):
        for copy in sent:
            copy.wait_recv()
            copy.wait_send()
        best = peaks[seg][...]
        for slot in range(len(sent)):
            best = jnp.maximum(best, arrivals[seg, slot, pl.ds(0, peaks[seg].shape[0]), :])
        peaks[seg][...] = best

    eye = lax.broadcasted_iota(jnp.int32, (LANES, LANES), 0) == lax.broadcasted_iota(
        jnp.int32, (LANES, LANES), 1
    )
    ones = jnp.ones((3 * LANES, LANES), jnp.bfloat16)

    def spread(seg):
        top = peaks[seg][...]
        whole = jnp.floor(top * (1.0 / 256.0))
        ratio = 32.0 / jnp.maximum(top, 1.0)
        near1 = ratio.astype(jnp.bfloat16).astype(jnp.float32)
        near2 = (ratio - near1).astype(jnp.bfloat16).astype(jnp.float32)
        parts = (whole * 8.0, (top - whole * 256.0) * (1.0 / 32.0), near1, near2, (ratio - near1) - near2)
        first, size = SEGMENTS[seg]
        padded = peaks[seg].shape[0] // 2
        for half in range(2):
            for r in range(size // 32):
                row = half * padded + r
                diag = [
                    jnp.where(eye, jnp.broadcast_to(part[row : row + 1, :], (LANES, LANES)), 0.0).astype(
                        jnp.bfloat16
                    )
                    for part in parts
                ]
                at = pl.ds(half * 2048 + first * 4 + r * LANES, LANES)
                high_all[at, :] = jnp.dot(diag[0], ones[:LANES], preferred_element_type=jnp.float32)
                low_all[at, :] = jnp.dot(diag[1], ones[:LANES], preferred_element_type=jnp.float32)
                ratio_all[at, :] = jnp.dot(
                    jnp.concatenate(diag[2:], axis=1), ones, preferred_element_type=jnp.float32
                )

    def quantize(peak_row, gap_table, point_table, sibling_row=None):
        keys = [(r, m, p) for r in range(PEAK_ROWS) for m in range(16) for p in (0, 1)]
        batches = [keys[i : i + BATCH] for i in range(0, len(keys), BATCH)]
        held = {}

        def find_cells(batch):
            for r, m, p in batch:
                at = rows_of((peak_row + r) * 16 + m, 1)
                value = (coef_even, coef_odd)[p][at, :]
                place = jnp.minimum((value * ratio_all[at, :] + 32.0).astype(jnp.int32), 63)
                held[r, m, p] = (value, place, take(gap_table, place))

        def round_cells(batch):
            for r, m, p in batch:
                at = rows_of((peak_row + r) * 16 + m, 1)
                value, place, packed = held[r, m, p]
                offset = dither_v[pl.ds((peak_row + r) * 256 + (16 * m + p), UNIT, stride=2), :]
                whole = jnp.floor(packed)
                bound = whole + offset.astype(jnp.float32) * (packed - whole)
                up = (value - high_all[at, :] * bound) > low_all[at, :] * bound
                held[r, m, p] = take(point_table, jnp.where(up, place + 64, place))

        def store(batch):
            for r, m, p in batch:
                code = held.pop((r, m, p))
                if sibling_row is not None:
                    near = pl.ds((sibling_row + r) * 256 + (16 * m + p), UNIT, stride=2)
                    code = code + sibling_in[near, :]
                codes[pl.ds((peak_row + r) * 256 + (16 * m + p), UNIT, stride=2), :] = code

        for i in range(len(batches) + 2):
            if i < len(batches):
                find_cells(batches[i])
            if 0 <= i - 1 < len(batches):
                round_cells(batches[i - 1])
            if i >= 2:
                store(batches[i - 2])

    def tables():
        cell = (lane & 63) - 32
        low = jnp.full((UNIT, LANES), level_values[0], jnp.int32)
        high = jnp.full((UNIT, LANES), level_values[1], jnp.int32)
        low_point = jnp.full((UNIT, LANES), level_points[0], jnp.float32)
        high_point = jnp.full((UNIT, LANES), level_points[1], jnp.float32)
        for j in range(1, 15):
            passed = cell >= level_values[j]
            low = jnp.where(passed, level_values[j], low)
            high = jnp.where(passed, level_values[j + 1], high)
            low_point = jnp.where(passed, level_points[j], low_point)
            high_point = jnp.where(passed, level_points[j + 1], high_point)
        gap = low.astype(jnp.float32) + (high - low).astype(jnp.float32) * (1.0 / 64.0)
        return gap, jnp.where(lane < 64, low_point, high_point)

    halves = [None] * 3

    def quantize_other(seg, gap_table, point_table):
        first, size = SEGMENTS[seg]

        def body(r, carry):
            quantize((theirs + first) // 32 + r * PEAK_ROWS, gap_table, point_table)
            return carry

        lax.fori_loop(0, size // 32 // PEAK_ROWS, body, 0)
        halves[seg] = copies.start(
            codes.at[rows_of(theirs + first, size)], sibling_in.at[rows_of(first, size)], sibling
        )

    def quantize_own(seg, gap_table, point_table):
        first, size = SEGMENTS[seg]
        halves[seg].wait_recv()

        def body(r, carry):
            quantize(
                (mine + first) // 32 + r * PEAK_ROWS, gap_table, point_table, first // 32 + r * PEAK_ROWS
            )
            return carry

        lax.fori_loop(0, size // 32 // PEAK_ROWS, body, 0)

    places, _ = layout()
    ring = {}

    def land(seg, name, skip, count):
        return landing.at[rows_of(places[seg, name][0] + skip, count)]

    def cut(seg):
        first, size = SEGMENTS[seg]
        quarter = size // RING
        axis = ORDERS[seg][0]
        part = [mine + first + lax.rem(here.at[axis] + d, RING) * quarter for d in range(RING)]
        return quarter, quarter // 2, part, here.near((axis, 1)), here.near((axis, 3))

    def scatter_first(seg):
        quarter, low, part, right, left = cut(seg)
        high = quarter - low
        ring[seg] = [
            copies.start(codes.at[rows_of(part[2], low)], land(seg, "tl", 0, low), right),
            copies.start(codes.at[rows_of(part[2] + low, high)], land(seg, "th", 0, high), left),
            copies.start(codes.at[rows_of(part[1] + low, high)], land(seg, "fa", low, high), right),
            copies.start(codes.at[rows_of(part[3], low)], land(seg, "fb", 0, low), left),
        ]

    def scatter_second(seg):
        quarter, low, part, right, left = cut(seg)
        high = quarter - low
        waits = ring[seg]
        waits[0].wait_recv()
        add_into(codes, part[1], [(landing, places[seg, "tl"][0])], low)
        waits.append(copies.start(codes.at[rows_of(part[1], low)], land(seg, "fa", 0, low), right))
        waits[1].wait_recv()
        add_into(codes, part[3] + low, [(landing, places[seg, "th"][0])], high)
        waits.append(copies.start(codes.at[rows_of(part[3] + low, high)], land(seg, "fb", low, high), left))

    plane = {}

    def piece_at(seg, i, j):
        quarter, _, part, _, _ = cut(seg)
        _, first, second = ORDERS[seg]
        spot = lax.rem(here.at[first] + i, RING) * RING + lax.rem(here.at[second] + j, RING)
        return part[0] + spot * (quarter // 16)

    def plane_partner(seg, i, j):
        _, first, second = ORDERS[seg]
        return here.near((first, i), (second, j))

    def scatter_plane(seg):
        quarter, _, part, _, _ = cut(seg)
        for copy in ring[seg][2:]:
            copy.wait_recv()
        add_into(codes, part[0], [(landing, places[seg, "fa"][0]), (landing, places[seg, "fb"][0])], quarter)
        piece = quarter // 16
        plane[seg] = [
            copies.start(
                codes.at[rows_of(piece_at(seg, i, j), piece)],
                land(seg, "plane", (i * RING + j) * piece, piece),
                plane_partner(seg, i, j),
            )
            for i, j in PLANE
        ]

    def scatter_last(seg):
        piece = SEGMENTS[seg][1] // 64
        for copy in plane[seg]:
            copy.wait_recv()
        first = places[seg, "plane"][0]
        add_into(
            codes,
            piece_at(seg, 0, 0),
            [(landing, first + (i * RING + j) * piece) for i, j in PLANE],
            piece,
        )

    small_loads[0].wait()
    for step in range(6):
        rotate(step)
    pl.semaphore_wait(barrier, len(partners))
    sent_a = peak_send(0, PEAK_FIRST, first_in)
    for step in range(6, 12):
        rotate(step)
    peak_take(0, sent_a, first_in)
    sent_a = peak_send(0, PEAK_SECOND, second_in)
    sent_b = peak_send(1, PEAK_FIRST, first_in)
    for step in range(12, 16):
        rotate(step)
    sent_c = peak_send(2, PEAK_FIRST, first_in)
    for load in small_loads[1:]:
        load.wait()
    gap_table, point_table = tables()
    peak_take(1, sent_b, first_in)
    sent_b = peak_send(1, PEAK_SECOND, second_in)
    peak_take(2, sent_c, first_in)
    sent_c = peak_send(2, PEAK_SECOND, second_in)
    peak_take(0, sent_a, second_in)
    spread(0)
    quantize_other(0, gap_table, point_table)
    peak_take(1, sent_b, second_in)
    spread(1)
    quantize_other(1, gap_table, point_table)
    quantize_own(0, gap_table, point_table)
    scatter_first(0)
    peak_take(2, sent_c, second_in)
    spread(2)
    quantize_other(2, gap_table, point_table)
    quantize_own(1, gap_table, point_table)
    scatter_first(1)
    scatter_second(0)
    quantize_own(2, gap_table, point_table)
    scatter_first(2)
    scatter_second(1)
    scatter_plane(0)
    scatter_second(2)
    scatter_plane(1)
    scatter_plane(2)
    for seg in range(3):
        scatter_last(seg)

    units = [(seg, piece_at(seg, 0, 0) + i) for seg, (_, size) in enumerate(SEGMENTS) for i in range(size // 64)]
    for i, (_, unit) in enumerate(units):
        owned[pl.ds(i * UNIT, UNIT), :] = codes[rows_of(unit, 1), :]
    count = len(units) * UNIT // 2
    both = jnp.concatenate(
        [owned[pl.ds(0, count, stride=2), :], owned[pl.ds(1, count, stride=2), :]], axis=1
    )
    back = jnp.dot(both, had, precision=lax.Precision.HIGHEST, preferred_element_type=jnp.float32)
    owned[pl.ds(0, count, stride=2), :] = back[:, :LANES]
    owned[pl.ds(1, count, stride=2), :] = back[:, LANES:]
    for i, (seg, unit) in enumerate(units):
        wide = jnp.broadcast_to(words[pl.ds(lax.div(unit, 4), 1), :], (UNIT, LANES))
        word = take(wide, word_lane + 32 * lax.rem(unit, 4))
        spot = unit - (mine + SEGMENTS[seg][0])
        row = core * (peaks[seg].shape[0] // 2) + lax.div(spot, 32)
        wide = jnp.broadcast_to(peaks[seg][pl.ds(row, 1), :], (UNIT, LANES))
        factor = take(wide, 4 * lax.rem(spot, 32) + (sub >> 1)) * (1.0 / 2.0**29)
        grad = owned[pl.ds(i * UNIT, UNIT), :] * factor
        out[rows_of(unit, 1), :] = jnp.where((word << word_shift) < 0, -grad, grad)

    def send(start, size, to):
        at = rows_of(start, size)
        return copies.start(out.at[at], out.at[at], to)

    last = []
    gather = {}
    arrive = {}

    def gather_plane(seg):
        piece = SEGMENTS[seg][1] // 64
        for i, j in PLANE:
            arrive.setdefault((seg, (RING - i) % RING), []).append(
                send(piece_at(seg, 0, 0), piece, plane_partner(seg, i, j))
            )

    def group_of(seg, i):
        quarter, _, part, right, left = cut(seg)
        size = quarter // RING
        skip = lax.rem(here.at[ORDERS[seg][1]] + i, RING) * size
        return size, size // 2, [start + skip for start in part], right, left

    def gather_first(seg, i):
        for copy in arrive[seg, i]:
            copy.wait_recv()
        size, low, part, right, left = group_of(seg, i)
        high = size - low
        gather[seg, i] = [
            send(part[0], low, right),
            send(part[0] + low, high, left),
            send(part[0] + low, high, right),
            send(part[0], low, left),
        ]
        last.append(send(part[0], size, sibling))

    def gather_second(seg, i):
        size, low, part, right, left = group_of(seg, i)
        high = size - low
        waits = gather[seg, i]
        waits[0].wait_recv()
        waits.append(send(part[3], low, right))
        waits[1].wait_recv()
        waits.append(send(part[1] + low, high, left))
        waits[2].wait_recv()
        waits[3].wait_recv()
        last.append(send(part[3], size, sibling))
        last.append(send(part[1], size, sibling))

    def gather_last(seg, i):
        size, _, part, _, _ = group_of(seg, i)
        for copy in gather[seg, i][4:]:
            copy.wait_recv()
        last.append(send(part[2], size, sibling))

    for seg in range(3):
        gather_plane(seg)
    for turn in range(len(GROUPS) + 2):
        if turn < len(GROUPS):
            for seg in range(3):
                gather_first(seg, GROUPS[turn])
        if 0 <= turn - 1 < len(GROUPS):
            for seg in range(3):
                gather_second(seg, GROUPS[turn - 1])
        if turn >= 2:
            for seg in range(3):
                gather_last(seg, GROUPS[turn - 2])
    for copy in last:
        copy.wait_recv()
    for copy in copies.all[3 * 22 :]:
        copy.wait_send()


def mean_gradient(gradients, dither, sign_words, level_values, level_points):
    units = layout()[1]
    whole = pltpu.VMEM((ROWS, LANES), jnp.float32)
    half = pltpu.VMEM((HALF_ROWS, LANES), jnp.float32)
    anywhere = pl.BlockSpec(memory_space=pltpu.HBM)
    return pl.pallas_call(
        reduce_kernel,
        out_shape=jax.ShapeDtypeStruct((ROWS, LANES), jnp.float32),
        in_specs=[anywhere] * 5,
        out_specs=pl.BlockSpec(memory_space=pltpu.VMEM),
        scratch_shapes=[
            pltpu.VMEM((1, ROWS * LANES), jnp.bfloat16),
            pltpu.VMEM((ROWS, LANES), jnp.int32),
            pltpu.VMEM((ROWS // 32, LANES), jnp.int32),
            pltpu.SMEM((16,), jnp.int32),
            pltpu.SMEM((16,), jnp.float32),
            pltpu.VMEM((CHUNK, LANES), jnp.float32),
            half,
            half,
            whole,
            pltpu.VMEM((16, LANES), jnp.float32),
            pltpu.VMEM((16, LANES), jnp.float32),
            pltpu.VMEM((8, LANES), jnp.float32),
            pltpu.VMEM((3, 7, 16, LANES), jnp.float32),
            pltpu.VMEM((3, 15, 16, LANES), jnp.float32),
            half,
            half,
            half,
            half,
            pltpu.VMEM((units * UNIT, LANES), jnp.float32),
            pltpu.VMEM((64, LANES), jnp.float32),
            pltpu.SemaphoreType.DMA((COPIES,)),
            pltpu.SemaphoreType.DMA((COPIES,)),
            pltpu.SemaphoreType.DMA((ROWS // CHUNK,)),
            pltpu.SemaphoreType.DMA((4,)),
        ],
        compiler_params=pltpu.CompilerParams(
            collective_id=0, has_side_effects=True, vmem_limit_bytes=47 * 2**20
        ),
        cost_estimate=pl.CostEstimate(flops=2**31, bytes_accessed=12 * 2**20, transcendentals=0),
    )(
        gradients,
        dither.reshape(ROWS, LANES),
        sign_words.reshape(-1, LANES),
        level_values,
        level_points,
    )


def body(
    gradients, dither, sign_words, level_values, level_points, params, first_moment, second_moment
):
    mean_grad = mean_gradient(gradients, dither, sign_words, level_values, level_points).reshape(-1)
    new_first = beta_first * first_moment + (1.0 - beta_first) * mean_grad
    new_second = beta_second * second_moment + (1.0 - beta_second) * mean_grad * mean_grad
    update = new_first / bias_first / (jnp.sqrt(new_second / bias_second) + epsilon)
    new_params = params - step_rate * update
    return (new_params, new_first, new_second, update)


def solution(mesh):
    placed = (P(("dp", "outer"), None), P(("dp", "outer"), None), P(), P(), P(), P(), P(), P())
    return jax.shard_map(
        body, mesh=mesh, in_specs=placed, out_specs=(P(), P(), P(), P()), check_vma=False
    )
```

time: 101 us -> 84.6 us (0.84)
  Pallas kernels: 87.7 us -> 74.8 us
  local copies, waits for them, and re-layouts: 4.4 us -> 2.22 us
  other arithmetic: 8.29 us -> 6.75 us
    pallas_call x1, Pallas kernels: 87.7 us -> 74.8 us  [mean_gradient(): pl.pallas_call(reduce_kernel, out_shape=jax.ShapeDtypeStruct((ROWS, LANES...]
    unnamed x12, local copies, waits for them, and re-layouts: 4.4 us -> 2.22 us
    sub x1, other arithmetic: 8.29 us -> 6.75 us  [body(): new_params = params - step_rate * update]
where the time goes in v2:
time: 84.6 us; the launch traced here: 84.4 us
  Pallas kernels  74.8 us (88%)
  other arithmetic  6.75 us (8%)
  local copies, waits for them, and re-layouts  2.22 us (3%)
    pallas_call x1, Pallas kernels, mean_gradient(): pl.pallas_call(reduce_kernel, out_shape=jax.ShapeDtypeStruct((ROWS, LANES...  74.8 us
    sub x1, other arithmetic, body(): new_params = params - step_rate * update  6.75 us
    unnamed x12, local copies, waits for them, and re-layouts  2.22 us

profile of v2, /device:TPU:1, one launch (start us, length us, event | category | flops | bytes accessed | tf_op | source)
XLA Modules:
  0.0 84.4 jit_solution(13140076446133626131)
XLA Ops:
  0.6 0.0 copy-start
  0.6 0.9 %copy-done = s32[32768]{0:T(1024)S(1)} copy-done((s32[32768]{0:T(1024)S(1)}, s32[32768]{0:T(1024)}, u32[]{:S(2)}) %copy-start) | copy-done | bytes 131096
  1.5 0.0 copy-start.1
  1.5 0.7 copy-done.1
  2.2 0.0 copy-start.2
  2.2 0.7 copy-done.2
  2.9 0.0 copy-start.3
  2.9 0.0 copy-start.4
  2.9 0.0 copy-start.5
  2.9 74.8 %shard_map.111 = f32[8192,128]{1,0:T(8,128)S(1)} custom-call(bf16[1,1048576]{1,0:T(2,128)(2,1)} %grad_hbm.1, s32[8192,128]{1,0:T(8,128)} %bitcast.10, s32[256,128]{1,0:T(8,128)S(1)} %bitcast.9, s32[16]{0:T(128)S(1)} %copy-done.1, f32[16]{0:T(128)S(1)} %copy-done.2), custom_call_target="tpu_custom_call" | custom-call | flops 2147483648 | bytes 12582912 | tf_op jit(solution)/shard_map/pallas_call | solution.py:541
  77.6 0.0 copy-done.3
  77.7 0.0 copy-done.4
  77.7 0.0 copy-done.5
  77.7 6.8 %multiply_subtract_fusion = (f32[1048576]{0:T(1024)}, f32[1048576]{0:T(1024)}, f32[1048576]{0:T(1024)}, f32[1048576]{0:T(1024)}) fusion(f32[1048576]{0:T(1024)S(1)} %copy-done.3, f32[8192,128]{1,0:T(8,128)S(1)} %shard_map.111, f32[1048576]{0:T(1024)S(1)} %copy-done.4, f32[1048576]{0:T(1024)S(1)} %copy-done.5), kind=kLoop, calls=%fused_computation.4 | loop fusion | flops 13631488 | bytes 33554432 | tf_op jit(solution)/shard_map/sub | solution.py:592
Async XLA Ops:
  0.6 0.9 %copy-start = (s32[32768]{0:T(1024)S(1)}, s32[32768]{0:T(1024)}, u32[]{:S(2)}) copy-start(s32[32768]{0:T(1024)} %param.10) | copy-start | bytes 393220
  1.5 0.7 copy-start.1
  2.2 0.7 copy-start.2
  2.9 74.8 %copy-start.3 = (f32[1048576]{0:T(1024)S(1)}, f32[1048576]{0:T(1024)}, u32[]{:S(2)}) copy-start(f32[1048576]{0:T(1024)} %param.13) | copy-start | bytes 12582916
  2.9 74.8 %copy-start.4 = (f32[1048576]{0:T(1024)S(1)}, f32[1048576]{0:T(1024)}, u32[]{:S(2)}) copy-start(f32[1048576]{0:T(1024)} %param.14) | copy-start | bytes 12582916
  2.9 74.8 %copy-start.5 = (f32[1048576]{0:T(1024)S(1)}, f32[1048576]{0:T(1024)}, u32[]{:S(2)}) copy-start(f32[1048576]{0:T(1024)} %param.15) | copy-start | bytes 12582916

commit v3 on v2

--- a/solution.py
+++ b/solution.py
@@ -14,10 +14,10 @@
 RING = 4
 SEGMENTS = ((0, 192), (192, 192), (384, 128))
 ORDERS = (("x", "y", "z"), ("y", "z", "x"), ("z", "x", "y"))
+GROUPS = (0, 1, 3, 2)
 PLANE = tuple((i, j) for i in (2, 1, 3, 0) for j in (2, 1, 3, 0) if i + j)
-GROUPS = (0, 1, 3, 2)
 BATCH = 16
-PEAK_ROWS = 2
+STEP_ROWS = (3, 3, 2)
 
 beta_first = 0.9
 beta_second = 0.95
@@ -80,9 +80,14 @@
         return copy
 
 
-PEAK_FIRST = tuple((("x", i), ("core", j)) for i in (2, 1, 3, 0) for j in (1, 0) if i + j)
-PEAK_SECOND = tuple((("y", i), ("z", j)) for i, j in PLANE)
-COPIES = 3 * (7 + 15 + 1 + 6 + 15 + 15 + 4 * 10)
+PEAK_ROUNDS = (
+    tuple((("x", i), ("core", j)) for i in (2, 1, 3, 0) for j in (1, 0) if i + j),
+    tuple((("y", i),) for i in (2, 1, 3)),
+    tuple((("z", i),) for i in (2, 1, 3)),
+)
+PEAK_FIRST_SLOT = (0, 7, 10)
+PEAK_COPIES = 13
+COPIES = 3 * (PEAK_COPIES + 1 + 6 + 15 + 15 + 4 * 10)
 
 
 def layout():
@@ -122,7 +127,7 @@
 def reduce_kernel(
     grad_hbm, dither_hbm, words_hbm, values_hbm, points_hbm, out,
     grad_v, dither_v, words, level_values, level_points, signed, coef_even, coef_odd, codes,
-    peak_a, peak_b, peak_c, first_in, second_in, high_all, low_all, ratio_all,
+    peak_a, peak_b, peak_c, peak_in, high_all, low_all, ratio_all,
     sibling_in, landing, owned, send_sems, recv_sems, grad_sems, load_sems,
 ):
     here = Place()
@@ -131,6 +136,11 @@
     peaks = (peak_a, peak_b, peak_c)
     sibling = here.near(("core", 1))
     mine, theirs = core * 512, (1 - core) * 512
+
+    barrier = pltpu.get_barrier_semaphore()
+    partners = [here.near(*moves) for moves in PEAK_ROUNDS[0] + PEAK_ROUNDS[1] + PEAK_ROUNDS[2]]
+    for partner in partners:
+        pl.semaphore_signal(barrier, inc=1, device_id=partner, device_id_type=MESH)
 
     small_loads = [
         pltpu.make_async_copy(src, dst, load_sems.at[i])
@@ -149,17 +159,8 @@
         at = pl.ds(pl.multiple_of(chunk * span, span), span)
         loads.append(pltpu.make_async_copy(grad_hbm.at[:, at], grad_v.at[:, at], grad_sems.at[i]))
         loads[-1].start()
-    for load in small_loads[1:]:
+    for load in small_loads[1:3]:
         load.start()
-
-    barrier = pltpu.get_barrier_semaphore()
-    partners = [here.near(*moves) for moves in PEAK_FIRST + PEAK_SECOND]
-    for a1, a2 in (("z", "x"), ("x", "y")):
-        for i in (1, 2, 3):
-            for j in (1, 2, 3):
-                partners.append(here.near((a1, i), (a2, j)))
-    for partner in partners:
-        pl.semaphore_signal(barrier, inc=1, device_id=partner, device_id_type=MESH)
 
     lane = lax.broadcasted_iota(jnp.int32, (UNIT, LANES), 1)
     sub = lax.broadcasted_iota(jnp.int32, (UNIT, LANES), 0)
@@ -170,23 +171,19 @@
     for ref in peaks:
         ref[...] = jnp.zeros_like(ref)
 
-    def rotate(step):
-        seg, half, chunk, i = steps[step]
-        loads[step].wait()
-
-        def sign_rows(r, carry):
+    def sign_chunk(chunk, slot):
+        for r in range(CHUNK // 32):
             word_row = chunk * (CHUNK // 32) + r
             wide = jnp.broadcast_to(words[pl.ds(word_row, 1), :], (UNIT, LANES))
             for k in range(4):
                 word = take(wide, word_lane + 32 * k)
                 first = pl.multiple_of(word_row * 4096 + k * 1024, 1024)
                 grad = grad_v[:, pl.ds(first, 1024)].astype(jnp.float32).reshape(UNIT, LANES)
-                signed[rows_of(r * 4 + k, 1), :] = jnp.where((word << word_shift) < 0, -grad, grad)
-            return carry
-
-        lax.fori_loop(0, CHUNK // 32, sign_rows, 0, unroll=4)
-        even = signed[pl.ds(0, CHUNK // 2, stride=2), :]
-        odd = signed[pl.ds(1, CHUNK // 2, stride=2), :]
+                signed[slot, rows_of(r * 4 + k, 1), :] = jnp.where((word << word_shift) < 0, -grad, grad)
+
+    def rotate_chunk(seg, half_core, i, chunk, slot):
+        even = signed[slot, pl.ds(0, CHUNK // 2, stride=2), :]
+        odd = signed[slot, pl.ds(1, CHUNK // 2, stride=2), :]
         both = jnp.concatenate([even, odd], axis=1).astype(jnp.bfloat16)
         coeffs = jnp.dot(both, had_bf, preferred_element_type=jnp.float32)
         at = rows_of(chunk * 32, 32)
@@ -196,24 +193,50 @@
             had_bf, both, (((1,), (1,)), ((), ())), preferred_element_type=jnp.float32
         )
         top = jnp.max(jnp.abs(turned), axis=0, keepdims=True)
-        half_core = lax.div(half, 512)
         for j in range(2):
             row = half_core * (peaks[seg].shape[0] // 2) + (2 * i + j)
             peaks[seg][pl.ds(row, 1), :] = top[:, j * LANES : (j + 1) * LANES]
 
-    def peak_send(seg, partners_of, arrivals):
-        return [
-            copies.start(peaks[seg], arrivals.at[seg, slot, pl.ds(0, peaks[seg].shape[0])], here.near(*moves))
-            for slot, moves in enumerate(partners_of)
+    def rotate(seg):
+        first, size = SEGMENTS[seg]
+        count = size // 64
+        for (step_seg, *_), load in zip(steps, loads, strict=True):
+            if step_seg == seg:
+                load.wait()
+
+        def body(h, carry):
+            half_core = (1 - core) + h * (2 * core - 1)
+            start = half_core * 8 + first // 64
+            for i in range(count + 1):
+                if i < count:
+                    sign_chunk(start + i, i % 2)
+                if i >= 1:
+                    rotate_chunk(seg, half_core, i - 1, start + i - 1, (i - 1) % 2)
+            return carry
+
+        lax.fori_loop(0, 2, body, 0)
+
+    sent_peaks = {}
+
+    def peak_send(seg, turn):
+        size = peaks[seg].shape[0]
+        sent_peaks[seg, turn] = [
+            copies.start(
+                peaks[seg],
+                peak_in.at[seg, PEAK_FIRST_SLOT[turn] + slot, pl.ds(0, size)],
+                here.near(*moves),
+            )
+            for slot, moves in enumerate(PEAK_ROUNDS[turn])
         ]
 
-    def peak_take(seg, sent, arrivals):
-        for copy in sent:
+    def peak_take(seg, turn):
+        for copy in sent_peaks[seg, turn]:
             copy.wait_recv()
             copy.wait_send()
         best = peaks[seg][...]
-        for slot in range(len(sent)):
-            best = jnp.maximum(best, arrivals[seg, slot, pl.ds(0, peaks[seg].shape[0]), :])
+        for slot in range(len(PEAK_ROUNDS[turn])):
+            arrived = peak_in[seg, PEAK_FIRST_SLOT[turn] + slot, pl.ds(0, peaks[seg].shape[0]), :]
+            best = jnp.maximum(best, arrived)
         peaks[seg][...] = best
 
     eye = lax.broadcasted_iota(jnp.int32, (LANES, LANES), 0) == lax.broadcasted_iota(
@@ -246,8 +269,8 @@
                     jnp.concatenate(diag[2:], axis=1), ones, preferred_element_type=jnp.float32
                 )
 
-    def quantize(peak_row, gap_table, point_table, sibling_row=None):
-        keys = [(r, m, p) for r in range(PEAK_ROWS) for m in range(16) for p in (0, 1)]
+    def quantize(count, peak_row, gap_table, point_table, sibling_row=None):
+        keys = [(r, m, p) for r in range(count) for m in range(16) for p in (0, 1)]
         batches = [keys[i : i + BATCH] for i in range(0, len(keys), BATCH)]
         held = {}
 
@@ -303,27 +326,27 @@
 
     def quantize_other(seg, gap_table, point_table):
         first, size = SEGMENTS[seg]
+        step = STEP_ROWS[seg]
 
         def body(r, carry):
-            quantize((theirs + first) // 32 + r * PEAK_ROWS, gap_table, point_table)
+            quantize(step, (theirs + first) // 32 + r * step, gap_table, point_table)
             return carry
 
-        lax.fori_loop(0, size // 32 // PEAK_ROWS, body, 0)
+        lax.fori_loop(0, size // 32 // step, body, 0)
         halves[seg] = copies.start(
             codes.at[rows_of(theirs + first, size)], sibling_in.at[rows_of(first, size)], sibling
         )
 
     def quantize_own(seg, gap_table, point_table):
         first, size = SEGMENTS[seg]
+        step = STEP_ROWS[seg]
         halves[seg].wait_recv()
 
         def body(r, carry):
-            quantize(
-                (mine + first) // 32 + r * PEAK_ROWS, gap_table, point_table, first // 32 + r * PEAK_ROWS
-            )
+            quantize(step, (mine + first) // 32 + r * step, gap_table, point_table, first // 32 + r * step)
             return carry
 
-        lax.fori_loop(0, size // 32 // PEAK_ROWS, body, 0)
+        lax.fori_loop(0, size // 32 // step, body, 0)
 
     places, _ = layout()
     ring = {}
@@ -399,35 +422,31 @@
         )
 
     small_loads[0].wait()
-    for step in range(6):
-        rotate(step)
+    rotate(0)
     pl.semaphore_wait(barrier, len(partners))
-    sent_a = peak_send(0, PEAK_FIRST, first_in)
-    for step in range(6, 12):
-        rotate(step)
-    peak_take(0, sent_a, first_in)
-    sent_a = peak_send(0, PEAK_SECOND, second_in)
-    sent_b = peak_send(1, PEAK_FIRST, first_in)
-    for step in range(12, 16):
-        rotate(step)
-    sent_c = peak_send(2, PEAK_FIRST, first_in)
+    peak_send(0, 0)
+    small_loads[3].start()
+    rotate(1)
+    peak_send(1, 0)
+    rotate(2)
+    peak_send(2, 0)
     for load in small_loads[1:]:
         load.wait()
     gap_table, point_table = tables()
-    peak_take(1, sent_b, first_in)
-    sent_b = peak_send(1, PEAK_SECOND, second_in)
-    peak_take(2, sent_c, first_in)
-    sent_c = peak_send(2, PEAK_SECOND, second_in)
-    peak_take(0, sent_a, second_in)
+    for turn in (0, 1):
+        for seg in range(3):
+            peak_take(seg, turn)
+            peak_send(seg, turn + 1)
+    peak_take(0, 2)
     spread(0)
     quantize_other(0, gap_table, point_table)
-    peak_take(1, sent_b, second_in)
+    peak_take(1, 2)
     spread(1)
-    quantize_other(1, gap_table, point_table)
+    peak_take(2, 2)
+    spread(2)
     quantize_own(0, gap_table, point_table)
     scatter_first(0)
-    peak_take(2, sent_c, second_in)
-    spread(2)
+    quantize_other(1, gap_table, point_table)
     quantize_other(2, gap_table, point_table)
     quantize_own(1, gap_table, point_table)
     scatter_first(1)
@@ -470,12 +489,13 @@
     gather = {}
     arrive = {}
 
-    def gather_plane(seg):
+    def gather_plane(seg, i):
         piece = SEGMENTS[seg][1] // 64
-        for i, j in PLANE:
-            arrive.setdefault((seg, (RING - i) % RING), []).append(
-                send(piece_at(seg, 0, 0), piece, plane_partner(seg, i, j))
-            )
+        for j in (2, 1, 3, 0):
+            if i + j:
+                arrive.setdefault((seg, (RING - i) % RING), []).append(
+                    send(piece_at(seg, 0, 0), piece, plane_partner(seg, i, j))
+                )
 
     def group_of(seg, i):
         quarter, _, part, right, left = cut(seg)
@@ -515,8 +535,9 @@
             copy.wait_recv()
         last.append(send(part[2], size, sibling))
 
-    for seg in range(3):
-        gather_plane(seg)
+    for i in GROUPS:
+        for seg in range(3):
+            gather_plane(seg, i)
     for turn in range(len(GROUPS) + 2):
         if turn < len(GROUPS):
             for seg in range(3):
@@ -529,7 +550,7 @@
                 gather_last(seg, GROUPS[turn - 2])
     for copy in last:
         copy.wait_recv()
-    for copy in copies.all[3 * 22 :]:
+    for copy in copies.all[3 * PEAK_COPIES :]:
         copy.wait_send()
 
 
@@ -549,15 +570,14 @@
             pltpu.VMEM((ROWS // 32, LANES), jnp.int32),
             pltpu.SMEM((16,), jnp.int32),
             pltpu.SMEM((16,), jnp.float32),
-            pltpu.VMEM((CHUNK, LANES), jnp.float32),
+            pltpu.VMEM((2, CHUNK, LANES), jnp.float32),
             half,
             half,
             whole,
             pltpu.VMEM((16, LANES), jnp.float32),
             pltpu.VMEM((16, LANES), jnp.float32),
             pltpu.VMEM((8, LANES), jnp.float32),
-            pltpu.VMEM((3, 7, 16, LANES), jnp.float32),
-            pltpu.VMEM((3, 15, 16, LANES), jnp.float32),
+            pltpu.VMEM((3, PEAK_COPIES, 16, LANES), jnp.float32),
             half,
             half,
             half,
@@ -588,7 +608,7 @@
     mean_grad = mean_gradient(gradients, dither, sign_words, level_values, level_points).reshape(-1)
     new_first = beta_first * first_moment + (1.0 - beta_first) * mean_grad
     new_second = beta_second * second_moment + (1.0 - beta_second) * mean_grad * mean_grad
-    update = new_first / bias_first / (jnp.sqrt(new_second / bias_second) + epsilon)
+    update = new_first * (1.0 / bias_first) / (jnp.sqrt(new_second * (1.0 / bias_second)) + epsilon)
     new_params = params - step_rate * update
     return (new_params, new_first, new_second, update)
 

time: 84.6 us -> 81.8 us (0.967)
  Pallas kernels: 74.8 us -> 72 us
    pallas_call x1, Pallas kernels: 74.8 us -> 72 us  [mean_gradient(): pl.pallas_call(reduce_kernel, out_shape=jax.ShapeDtypeStruct((ROWS, LANES...]
where the time goes in v3:
time: 81.8 us; the launch traced here: 81.7 us
  Pallas kernels  72 us (88%)
  other arithmetic  6.75 us (8%)
  local copies, waits for them, and re-layouts  2.22 us (3%)
    pallas_call x1, Pallas kernels, mean_gradient(): pl.pallas_call(reduce_kernel, out_shape=jax.ShapeDtypeStruct((ROWS, LANES...  72 us
    sub x1, other arithmetic, body(): new_params = params - step_rate * update  6.75 us
    unnamed x12, local copies, waits for them, and re-layouts  2.22 us

profile of v3, /device:TPU:1, one launch (start us, length us, event | category | flops | bytes accessed | tf_op | source)
XLA Modules:
  0.0 81.7 jit_solution(9911136003130193012)
XLA Ops:
  0.6 0.0 copy-start
  0.6 0.9 %copy-done = s32[32768]{0:T(1024)S(1)} copy-done((s32[32768]{0:T(1024)S(1)}, s32[32768]{0:T(1024)}, u32[]{:S(2)}) %copy-start) | copy-done | bytes 131096
  1.5 0.0 copy-start.1
  1.5 0.7 copy-done.1
  2.2 0.0 copy-start.2
  2.2 0.7 copy-done.2
  2.9 0.0 copy-start.3
  2.9 0.0 copy-start.4
  2.9 0.0 copy-start.5
  2.9 72.0 %shard_map.111 = f32[8192,128]{1,0:T(8,128)S(1)} custom-call(bf16[1,1048576]{1,0:T(2,128)(2,1)} %grad_hbm.1, s32[8192,128]{1,0:T(8,128)} %bitcast.10, s32[256,128]{1,0:T(8,128)S(1)} %bitcast.9, s32[16]{0:T(128)S(1)} %copy-done.1, f32[16]{0:T(128)S(1)} %copy-done.2), custom_call_target="tpu_custom_call" | custom-call | flops 2147483648 | bytes 12582912 | tf_op jit(solution)/shard_map/pallas_call | solution.py:562
  74.9 0.0 copy-done.3
  74.9 0.0 copy-done.4
  74.9 0.0 copy-done.5
  74.9 6.8 %multiply_subtract_fusion = (f32[1048576]{0:T(1024)}, f32[1048576]{0:T(1024)}, f32[1048576]{0:T(1024)}, f32[1048576]{0:T(1024)}) fusion(f32[1048576]{0:T(1024)S(1)} %copy-done.3, f32[8192,128]{1,0:T(8,128)S(1)} %shard_map.111, f32[1048576]{0:T(1024)S(1)} %copy-done.4, f32[1048576]{0:T(1024)S(1)} %copy-done.5), kind=kLoop, calls=%fused_computation.4 | loop fusion | flops 13631488 | bytes 33554432 | tf_op jit(solution)/shard_map/sub | solution.py:612
Async XLA Ops:
  0.6 0.9 %copy-start = (s32[32768]{0:T(1024)S(1)}, s32[32768]{0:T(1024)}, u32[]{:S(2)}) copy-start(s32[32768]{0:T(1024)} %param.10) | copy-start | bytes 393220
  1.5 0.7 copy-start.1
  2.2 0.7 copy-start.2
  2.9 72.1 %copy-start.3 = (f32[1048576]{0:T(1024)S(1)}, f32[1048576]{0:T(1024)}, u32[]{:S(2)}) copy-start(f32[1048576]{0:T(1024)} %param.13) | copy-start | bytes 12582916
  2.9 72.1 %copy-start.4 = (f32[1048576]{0:T(1024)S(1)}, f32[1048576]{0:T(1024)}, u32[]{:S(2)}) copy-start(f32[1048576]{0:T(1024)} %param.14) | copy-start | bytes 12582916
  2.9 72.1 %copy-start.5 = (f32[1048576]{0:T(1024)S(1)}, f32[1048576]{0:T(1024)}, u32[]{:S(2)}) copy-start(f32[1048576]{0:T(1024)} %param.15) | copy-start | bytes 12582916

commit v4 on v0

v4 whole, which is shorter than its diff:
```python
import jax
import jax.numpy as jnp
from jax import lax
from jax.experimental import pallas as pl
from jax.experimental.pallas import tpu as pltpu
from jax.sharding import PartitionSpec as P

MESH = pl.DeviceIdType.MESH
LANES = 128
UNIT = 8
ROWS = 8192
CHUNK = 512
RING = 4
PARTS = 8
ORDERS = (("x", "y", "z"), ("y", "z", "x"), ("z", "x", "y"))
MEMBERS = ((0, 3), (3, 3), (6, 2))
WAVES = ((0, 3, 6), (1, 4, 7), (2, 5))
QUARTER = 16
GROUPS = (0, 1, 3, 2)
PLANE = tuple((i, j) for i in (2, 1, 3, 0) for j in (2, 1, 3, 0) if i + j)
BATCH = 16

beta_first = 0.9
beta_second = 0.95
bias_first = 1.0 - 0.9**50
bias_second = 1.0 - 0.95**50
epsilon = 1e-08
step_rate = 0.01


def rows_of(start, count):
    return pl.ds(pl.multiple_of(start * UNIT, UNIT), count * UNIT)


def take(table, idx):
    return jnp.take_along_axis(table, idx, axis=1, mode="promise_in_bounds")


def hadamard_128(length):
    common = lax.broadcasted_iota(jnp.int32, (length, length), 0) & lax.broadcasted_iota(
        jnp.int32, (length, length), 1
    )
    for shift in (4, 2, 1):
        common = common ^ (common >> shift)
    return jnp.where((common & 1) == 1, -128.0, 128.0).astype(jnp.float32)


class Place:
    def __init__(self):
        dp, outer = lax.axis_index("dp"), lax.axis_index("outer")
        self.at = {
            "y": lax.div(dp, 8),
            "x": lax.rem(lax.div(dp, 4), 2) * 2 + lax.div(outer, 2),
            "z": lax.rem(dp, 4),
            "core": lax.rem(outer, 2),
        }

    def near(self, *moves):
        at = dict(self.at)
        for axis, delta in moves:
            at[axis] = lax.rem(at[axis] + delta, 2 if axis == "core" else RING)
        dp = at["y"] * 8 + lax.div(at["x"], 2) * 4 + at["z"]
        return {"dp": dp, "outer": lax.rem(at["x"], 2) * 2 + at["core"]}


class Copies:
    def __init__(self, send, recv):
        self.send, self.recv, self.used, self.late = send, recv, 0, []

    def start(self, src, dst, to, late=True):
        copy = pltpu.make_async_remote_copy(
            src_ref=src,
            dst_ref=dst,
            send_sem=self.send.at[self.used],
            recv_sem=self.recv.at[self.used],
            device_id=to,
            device_id_type=MESH,
        )
        self.used += 1
        if late:
            self.late.append(copy)
        copy.start()
        return copy


PEAK_ROUNDS = (
    tuple((("x", i), ("core", j)) for i in (2, 1, 3, 0) for j in (1, 0) if i + j),
    tuple((("y", i),) for i in (2, 1, 3)),
    tuple((("z", i),) for i in (2, 1, 3)),
)
PEAK_FIRST_SLOT = (0, 7, 10)
PEAK_COPIES = 13
COPIES = 3 * PEAK_COPIES + 1 + PARTS * (2 + 6 + 15) + 3 * (15 + 4 * 10)


LANDING = {"tl": 0, "th": 8, "fa": 16, "fb": 32, "plane": 48}
LANDING_UNITS = 64


def add_into(dst, part, start, landing, firsts, count):
    here = rows_of(start, count)
    value = dst[part, here, :]
    for first in firsts:
        value = value + landing[part, rows_of(first, count), :]
    dst[part, here, :] = value


def reduce_kernel(
    grad_hbm, dither_hbm, words_hbm, values_hbm, points_hbm, out,
    grad_v, dither_v, words, level_values, level_points, signed, coef_even, coef_odd, codes,
    peak_a, peak_b, peak_c, peak_in, high_all, low_all, ratio_all,
    near_even, near_odd, near_dither, landing, owned, send_sems, recv_sems, grad_sems, load_sems,
):
    here = Place()
    core = here.at["core"]
    copies = Copies(send_sems, recv_sems)
    peaks = (peak_a, peak_b, peak_c)
    sibling = here.near(("core", 1))
    mine, theirs = core * PARTS, (1 - core) * PARTS

    barrier = pltpu.get_barrier_semaphore()
    partners = [here.near(*moves) for moves in PEAK_ROUNDS[0] + PEAK_ROUNDS[1] + PEAK_ROUNDS[2]]
    for partner in partners:
        pl.semaphore_signal(barrier, inc=1, device_id=partner, device_id_type=MESH)

    small_loads = [
        pltpu.make_async_copy(src, dst, load_sems.at[i])
        for i, (src, dst) in enumerate(
            (
                (words_hbm, words),
                (values_hbm, level_values),
                (points_hbm, level_points),
                (dither_hbm.at[pl.ds(mine, PARTS)], dither_v),
            )
        )
    ]
    small_loads[0].start()
    span = CHUNK * LANES
    loads = [[] for _ in WAVES]
    for wave, parts in enumerate(WAVES):
        for i, part in enumerate(parts):
            for j, half in enumerate((theirs, mine)):
                at = pl.ds(pl.multiple_of((half + part) * span, span), span)
                loads[wave].append(
                    pltpu.make_async_copy(grad_hbm.at[:, at], grad_v.at[:, at], grad_sems.at[part * 2 + j])
                )
                loads[wave][-1].start()
    for load in small_loads[1:3]:
        load.start()

    lane = lax.broadcasted_iota(jnp.int32, (UNIT, LANES), 1)
    sub = lax.broadcasted_iota(jnp.int32, (UNIT, LANES), 0)
    word_lane = sub * 4 + (lane >> 5)
    word_shift = 31 - (lane & 31)
    had = hadamard_128(2 * LANES)
    had_bf = had.astype(jnp.bfloat16)
    for ref in peaks:
        ref[...] = jnp.zeros_like(ref)

    def sign_chunk(chunk, slot):
        for r in range(CHUNK // 32):
            word_row = chunk * (CHUNK // 32) + r
            wide = jnp.broadcast_to(words[pl.ds(word_row, 1), :], (UNIT, LANES))
            for k in range(4):
                word = take(wide, word_lane + 32 * k)
                first = pl.multiple_of(word_row * 4096 + k * 1024, 1024)
                grad = grad_v[:, pl.ds(first, 1024)].astype(jnp.float32).reshape(UNIT, LANES)
                signed[slot, rows_of(r * 4 + k, 1), :] = jnp.where((word << word_shift) < 0, -grad, grad)

    def rotate_chunk(wave, half_core, i, chunk, slot):
        even = signed[slot, pl.ds(0, CHUNK // 2, stride=2), :]
        odd = signed[slot, pl.ds(1, CHUNK // 2, stride=2), :]
        both = jnp.concatenate([even, odd], axis=1).astype(jnp.bfloat16)
        coeffs = jnp.dot(both, had_bf, preferred_element_type=jnp.float32)
        coef_even[chunk] = coeffs[:, :LANES]
        coef_odd[chunk] = coeffs[:, LANES:]
        turned = lax.dot_general(
            had_bf, both, (((1,), (1,)), ((), ())), preferred_element_type=jnp.float32
        )
        top = jnp.max(jnp.abs(turned), axis=0, keepdims=True)
        for j in range(2):
            peaks[wave][pl.ds(half_core * 8 + (2 * i + j), 1), :] = top[:, j * LANES : (j + 1) * LANES]

    def rotate(wave):
        for load in loads[wave]:
            load.wait()
        parts = WAVES[wave]

        def body(h, carry):
            half_core = (1 - core) + h * (2 * core - 1)
            for i in range(len(parts) + 1):
                if i < len(parts):
                    sign_chunk(half_core * PARTS + parts[i], i % 2)
                if i >= 1:
                    rotate_chunk(wave, half_core, i - 1, half_core * PARTS + parts[i - 1], (i - 1) % 2)
            return carry

        lax.fori_loop(0, 2, body, 0)

    near_copies = {}

    def share(wave):
        near_copies[wave] = []
        for part in WAVES[wave]:
            for src, dst in ((coef_even, near_even), (coef_odd, near_odd)):
                near_copies[wave].append(copies.start(src.at[theirs + part], dst.at[part], sibling))

    sent_peaks = {}

    def peak_send(wave, turn):
        sent_peaks[wave, turn] = [
            copies.start(
                peaks[wave], peak_in.at[wave, PEAK_FIRST_SLOT[turn] + slot], here.near(*moves), late=False
            )
            for slot, moves in enumerate(PEAK_ROUNDS[turn])
        ]

    def peak_take(wave, turn):
        for copy in sent_peaks[wave, turn]:
            copy.wait_recv()
            copy.wait_send()
        best = peaks[wave][...]
        for slot in range(len(PEAK_ROUNDS[turn])):
            best = jnp.maximum(best, peak_in[wave, PEAK_FIRST_SLOT[turn] + slot])
        peaks[wave][...] = best

    eye = lax.broadcasted_iota(jnp.int32, (LANES, LANES), 0) == lax.broadcasted_iota(
        jnp.int32, (LANES, LANES), 1
    )
    ones = jnp.ones((3 * LANES, LANES), jnp.bfloat16)

    def spread(wave):
        top = peaks[wave][rows_of(core, 1), :]
        whole = jnp.floor(top * (1.0 / 256.0))
        ratio = 32.0 / jnp.maximum(top, 1.0)
        near1 = ratio.astype(jnp.bfloat16).astype(jnp.float32)
        near2 = (ratio - near1).astype(jnp.bfloat16).astype(jnp.float32)
        pieces = (whole * 8.0, (top - whole * 256.0) * (1.0 / 32.0), near1, near2, (ratio - near1) - near2)
        for i, part in enumerate(WAVES[wave]):
            for j in range(2):
                row = 2 * i + j
                diag = [
                    jnp.where(eye, jnp.broadcast_to(piece[row : row + 1, :], (LANES, LANES)), 0.0).astype(
                        jnp.bfloat16
                    )
                    for piece in pieces
                ]
                at = pl.ds(j * LANES, LANES)
                high_all[part, at, :] = jnp.dot(diag[0], ones[:LANES], preferred_element_type=jnp.float32)
                low_all[part, at, :] = jnp.dot(diag[1], ones[:LANES], preferred_element_type=jnp.float32)
                ratio_all[part, at, :] = jnp.dot(
                    jnp.concatenate(diag[2:], axis=1), ones, preferred_element_type=jnp.float32
                )

    def tables():
        cell = (lane & 63) - 32
        low = jnp.full((UNIT, LANES), level_values[0], jnp.int32)
        high = jnp.full((UNIT, LANES), level_values[1], jnp.int32)
        low_point = jnp.full((UNIT, LANES), level_points[0], jnp.float32)
        high_point = jnp.full((UNIT, LANES), level_points[1], jnp.float32)
        for j in range(1, 15):
            passed = cell >= level_values[j]
            low = jnp.where(passed, level_values[j], low)
            high = jnp.where(passed, level_values[j + 1], high)
            low_point = jnp.where(passed, level_points[j], low_point)
            high_point = jnp.where(passed, level_points[j + 1], high_point)
        gap = low.astype(jnp.float32) + (high - low).astype(jnp.float32) * (1.0 / 64.0)
        return gap, jnp.where(lane < 64, low_point, high_point)

    def quantize_chunk(part, gap_table, point_table):
        keys = [(m, p, own) for m in range(CHUNK // 16) for p in (0, 1) for own in (True, False)]
        batches = [keys[i : i + BATCH] for i in range(0, len(keys), BATCH)]
        held = {}

        def find_cells(batch):
            for m, p, own in batch:
                at = rows_of(m, 1)
                if own:
                    value = (coef_even, coef_odd)[p][mine + part, at, :]
                else:
                    value = (near_even, near_odd)[p][part, at, :]
                place = jnp.minimum((value * ratio_all[part, at, :] + 32.0).astype(jnp.int32), 63)
                held[m, p, own] = (value, place, take(gap_table, place))

        def round_cells(batch):
            for m, p, own in batch:
                at = rows_of(m, 1)
                value, place, packed = held[m, p, own]
                offset = (dither_v if own else near_dither)[part, pl.ds(16 * m + p, UNIT, stride=2), :]
                whole = jnp.floor(packed)
                bound = whole + offset.astype(jnp.float32) * (packed - whole)
                up = (value - high_all[part, at, :] * bound) > low_all[part, at, :] * bound
                held[m, p, own] = take(point_table, jnp.where(up, place + 64, place))

        def store(batch):
            for m, p, own in batch:
                if own:
                    codes[part, pl.ds(16 * m + p, UNIT, stride=2), :] = held.pop((m, p, True)) + held.pop(
                        (m, p, False)
                    )

        for i in range(len(batches) + 2):
            if i < len(batches):
                find_cells(batches[i])
            if 0 <= i - 1 < len(batches):
                round_cells(batches[i - 1])
            if i >= 2:
                store(batches[i - 2])

    def quantize(wave, gap_table, point_table):
        for copy in near_copies[wave]:
            copy.wait_recv()
        parts = WAVES[wave]

        def body(i, carry):
            quantize_chunk(parts[0] + i * (parts[1] - parts[0]), gap_table, point_table)
            return carry

        lax.fori_loop(0, len(parts), body, 0)

    ring = {}

    def order_of(part):
        return ORDERS[part // 3]

    def quarters(order):
        return [lax.rem(here.at[order[0]] + d, RING) * QUARTER for d in range(RING)]

    def scatter_first(part):
        order = order_of(part)
        at = quarters(order)
        right, left = here.near((order[0], 1)), here.near((order[0], 3))

        def move(start, name, skip, to):
            return copies.start(
                codes.at[part, rows_of(start, 8)], landing.at[part, rows_of(LANDING[name] + skip, 8)], to
            )

        ring[part] = [
            move(at[2], "tl", 0, right),
            move(at[2] + 8, "th", 0, left),
            move(at[1] + 8, "fa", 8, right),
            move(at[3], "fb", 0, left),
        ]

    def scatter_second(part):
        order = order_of(part)
        at = quarters(order)
        right, left = here.near((order[0], 1)), here.near((order[0], 3))
        waits = ring[part]
        waits[0].wait_recv()
        add_into(codes, part, at[1], landing, [LANDING["tl"]], 8)
        waits.append(
            copies.start(codes.at[part, rows_of(at[1], 8)], landing.at[part, rows_of(LANDING["fa"], 8)], right)
        )
        waits[1].wait_recv()
        add_into(codes, part, at[3] + 8, landing, [LANDING["th"]], 8)
        waits.append(
            copies.start(
                codes.at[part, rows_of(at[3] + 8, 8)], landing.at[part, rows_of(LANDING["fb"] + 8, 8)], left
            )
        )

    plane = {}

    def piece_at(order, i, j):
        spot = lax.rem(here.at[order[1]] + i, RING) * RING + lax.rem(here.at[order[2]] + j, RING)
        return here.at[order[0]] * QUARTER + spot

    def scatter_plane(part):
        order = order_of(part)
        for copy in ring[part][2:]:
            copy.wait_recv()
        add_into(
            codes, part, here.at[order[0]] * QUARTER, landing, [LANDING["fa"], LANDING["fb"]], QUARTER
        )
        plane[part] = [
            copies.start(
                codes.at[part, rows_of(piece_at(order, i, j), 1)],
                landing.at[part, rows_of(LANDING["plane"] + i * RING + j, 1)],
                here.near((order[1], i), (order[2], j)),
            )
            for i, j in PLANE
        ]

    def scatter_last(part):
        for copy in plane[part]:
            copy.wait_recv()
        firsts = [LANDING["plane"] + i * RING + j for i, j in PLANE]
        add_into(codes, part, piece_at(order_of(part), 0, 0), landing, firsts, 1)

    small_loads[0].wait()
    rotate(0)
    pl.semaphore_wait(barrier, len(partners))
    peak_send(0, 0)
    small_loads[3].start()
    near_dither_copy = copies.start(dither_hbm.at[pl.ds(theirs, PARTS)], near_dither, sibling)
    share(0)
    rotate(1)
    peak_send(1, 0)
    share(1)
    rotate(2)
    peak_send(2, 0)
    share(2)
    for load in small_loads[1:]:
        load.wait()
    gap_table, point_table = tables()
    for turn in (0, 1):
        for wave in range(3):
            peak_take(wave, turn)
            peak_send(wave, turn + 1)
    near_dither_copy.wait_recv()
    for wave in range(3):
        peak_take(wave, 2)
        spread(wave)
        quantize(wave, gap_table, point_table)
        for part in WAVES[wave]:
            scatter_first(part)
    for part in WAVES[0] + WAVES[1]:
        scatter_second(part)
    for part in WAVES[0]:
        scatter_plane(part)
    for part in WAVES[2]:
        scatter_second(part)
    for part in WAVES[1] + WAVES[2]:
        scatter_plane(part)
    for part in range(PARTS):
        scatter_last(part)

    for part in range(PARTS):
        owned[pl.ds(part * UNIT, UNIT), :] = codes[part, rows_of(piece_at(order_of(part), 0, 0), 1), :]
    count = PARTS * UNIT // 2
    both = jnp.concatenate(
        [owned[pl.ds(0, count, stride=2), :], owned[pl.ds(1, count, stride=2), :]], axis=1
    )
    back = jnp.dot(both, had, precision=lax.Precision.HIGHEST, preferred_element_type=jnp.float32)
    owned[pl.ds(0, count, stride=2), :] = back[:, :LANES]
    owned[pl.ds(1, count, stride=2), :] = back[:, LANES:]
    for wave, parts in enumerate(WAVES):
        for i, part in enumerate(parts):
            spot = piece_at(order_of(part), 0, 0)
            word_row = (mine + part) * (CHUNK // 32) + lax.div(spot, 4)
            wide = jnp.broadcast_to(words[pl.ds(word_row, 1), :], (UNIT, LANES))
            word = take(wide, word_lane + 32 * lax.rem(spot, 4))
            row = core * 8 + 2 * i + lax.div(spot, 32)
            wide = jnp.broadcast_to(peaks[wave][pl.ds(row, 1), :], (UNIT, LANES))
            factor = take(wide, 4 * lax.rem(spot, 32) + (sub >> 1)) * (1.0 / 2.0**29)
            grad = owned[pl.ds(part * UNIT, UNIT), :] * factor
            out[mine + part, rows_of(spot, 1), :] = jnp.where((word << word_shift) < 0, -grad, grad)

    last = []
    gather = {}
    arrive = {}

    def send(turn, start, size, to):
        first, count = MEMBERS[turn]
        at = out.at[pl.ds(mine + first, count), rows_of(start, size)]
        return copies.start(at, at, to)

    def gather_plane(turn, i):
        order = ORDERS[turn]
        for j in (2, 1, 3, 0):
            if i + j:
                arrive.setdefault((turn, (RING - i) % RING), []).append(
                    send(turn, piece_at(order, 0, 0), 1, here.near((order[1], i), (order[2], j)))
                )

    def group_of(turn, i):
        order = ORDERS[turn]
        skip = lax.rem(here.at[order[1]] + i, RING) * RING
        starts = [start + skip for start in quarters(order)]
        return starts, here.near((order[0], 1)), here.near((order[0], 3))

    def gather_first(turn, i):
        for copy in arrive[turn, i]:
            copy.wait_recv()
        at, right, left = group_of(turn, i)
        gather[turn, i] = [
            send(turn, at[0], 2, right),
            send(turn, at[0] + 2, 2, left),
            send(turn, at[0] + 2, 2, right),
            send(turn, at[0], 2, left),
        ]
        last.append(send(turn, at[0], RING, sibling))

    def gather_second(turn, i):
        at, right, left = group_of(turn, i)
        waits = gather[turn, i]
        waits[0].wait_recv()
        waits.append(send(turn, at[3], 2, right))
        waits[1].wait_recv()
        waits.append(send(turn, at[1] + 2, 2, left))
        waits[2].wait_recv()
        waits[3].wait_recv()
        last.append(send(turn, at[3], RING, sibling))
        last.append(send(turn, at[1], RING, sibling))

    def gather_last(turn, i):
        at, _, _ = group_of(turn, i)
        for copy in gather[turn, i][4:]:
            copy.wait_recv()
        last.append(send(turn, at[2], RING, sibling))

    for i in GROUPS:
        for turn in range(3):
            gather_plane(turn, i)
    for step in range(len(GROUPS) + 2):
        if step < len(GROUPS):
            for turn in range(3):
                gather_first(turn, GROUPS[step])
        if 0 <= step - 1 < len(GROUPS):
            for turn in range(3):
                gather_second(turn, GROUPS[step - 1])
        if step >= 2:
            for turn in range(3):
                gather_last(turn, GROUPS[step - 2])
    for copy in last:
        copy.wait_recv()
    for copy in copies.late:
        copy.wait_send()


def mean_gradient(gradients, dither, sign_words, level_values, level_points):
    chunks = 2 * PARTS
    whole = pltpu.VMEM((chunks, CHUNK // 2, LANES), jnp.float32)
    quarter = pltpu.VMEM((PARTS, CHUNK // 2, LANES), jnp.float32)
    peak = pltpu.VMEM((16, LANES), jnp.float32)
    anywhere = pl.BlockSpec(memory_space=pltpu.HBM)
    return pl.pallas_call(
        reduce_kernel,
        out_shape=jax.ShapeDtypeStruct((chunks, CHUNK, LANES), jnp.float32),
        in_specs=[anywhere] * 5,
        out_specs=pl.BlockSpec(memory_space=pltpu.VMEM),
        scratch_shapes=[
            pltpu.VMEM((1, ROWS * LANES), jnp.bfloat16),
            pltpu.VMEM((PARTS, CHUNK, LANES), jnp.int32),
            pltpu.VMEM((ROWS // 32, LANES), jnp.int32),
            pltpu.SMEM((16,), jnp.int32),
            pltpu.SMEM((16,), jnp.float32),
            pltpu.VMEM((2, CHUNK, LANES), jnp.float32),
            whole,
            whole,
            pltpu.VMEM((PARTS, CHUNK, LANES), jnp.float32),
            peak,
            peak,
            peak,
            pltpu.VMEM((3, PEAK_COPIES, 16, LANES), jnp.float32),
            quarter,
            quarter,
            quarter,
            quarter,
            quarter,
            pltpu.VMEM((PARTS, CHUNK, LANES), jnp.int32),
            pltpu.VMEM((PARTS, LANDING_UNITS * UNIT, LANES), jnp.float32),
            pltpu.VMEM((PARTS * UNIT, LANES), jnp.float32),
            pltpu.SemaphoreType.DMA((COPIES,)),
            pltpu.SemaphoreType.DMA((COPIES,)),
            pltpu.SemaphoreType.DMA((chunks,)),
            pltpu.SemaphoreType.DMA((4,)),
        ],
        compiler_params=pltpu.CompilerParams(
            collective_id=0, has_side_effects=True, vmem_limit_bytes=47 * 2**20
        ),
        cost_estimate=pl.CostEstimate(flops=2**31, bytes_accessed=12 * 2**20, transcendentals=0),
    )(
        gradients,
        dither.reshape(chunks, CHUNK, LANES),
        sign_words.reshape(-1, LANES),
        level_values,
        level_points,
    )


def body(
    gradients, dither, sign_words, level_values, level_points, params, first_moment, second_moment
):
    mean_grad = mean_gradient(gradients, dither, sign_words, level_values, level_points).reshape(-1)
    new_first = beta_first * first_moment + (1.0 - beta_first) * mean_grad
    new_second = beta_second * second_moment + (1.0 - beta_second) * mean_grad * mean_grad
    update = new_first * (1.0 / bias_first) / (jnp.sqrt(new_second * (1.0 / bias_second)) + epsilon)
    new_params = params - step_rate * update
    return (new_params, new_first, new_second, update)


def solution(mesh):
    placed = (P(("dp", "outer"), None), P(("dp", "outer"), None), P(), P(), P(), P(), P(), P())
    return jax.shard_map(
        body, mesh=mesh, in_specs=placed, out_specs=(P(), P(), P(), P()), check_vma=False
    )
```

time: 570 us -> 78.9 us (0.14)
  waiting for transfers between devices: 275 us -> 0 us
  other arithmetic: 147 us -> 6.75 us
  Pallas kernels: 0 us -> 69.1 us
  blocking collectives: 68.8 us -> 0 us
  local copies, waits for them, and re-layouts: 46.7 us -> 2.22 us
  matrix products: 17.3 us -> 0 us
  between operations: 13.8 us -> 0.68 us
    reduce_scatter x1 -> x0, waiting for transfers between devices: 165 us -> none  [body(): lax.psum_scatter(code_vals, 'dp', scatter_dimension=0, tiled=True)]
    pallas_call x0 -> x1, Pallas kernels: none -> 69.1 us  [mean_gradient(): pl.pallas_call(reduce_kernel, out_shape=jax.ShapeDtypeStruct((chunks, CHU...]
    pmax x1 -> x0, blocking collectives: 68.8 us -> none  [body(): peak_vals = lax.pmax(jnp.max(jnp.abs(coeffs), axis=1), ('dp', 'outer'))]
    psum x1 -> x0, waiting for transfers between devices: 56.4 us -> none  [body(): owned_sums = lax.psum(owned_sums, 'outer')]
    mul x2 -> x0, other arithmetic: 55.2 us -> none  [the longest x1 46.3 us: rotate(): grad_row.astype(jnp.float32) * 128.0 * sign_vals.astype(jnp.float32)]
    all_gather x1 -> x0, waiting for transfers between devices: 53.1 us -> none  [body(): all_sums = lax.all_gather(owned_sums, 'dp', axis=0, tiled=True)]
    unnamed x1 -> x0, other arithmetic: 34.2 us -> none
    select_n x1 -> x0, other arithmetic: 33.1 us -> none  [quantize(): return jnp.where(rounds_up, upper_point, lower_point)]
  transfers between devices with their start and end apart: 3 -> 0, of which waited for: 3 -> 0; matrix products, arithmetic and copies ran while one was open for 5% -> 0% of each run, Pallas kernels for 0% -> 0%
where the time goes in v4:
time: 78.9 us; the launch traced here: 78.8 us
  Pallas kernels  69.1 us (88%)
  other arithmetic  6.75 us (9%)
  local copies, waits for them, and re-layouts  2.22 us (3%)
    pallas_call x1, Pallas kernels, mean_gradient(): pl.pallas_call(reduce_kernel, out_shape=jax.ShapeDtypeStruct((chunks, CHU...  69.1 us
    sub x1, other arithmetic, body(): new_params = params - step_rate * update  6.75 us
    unnamed x12, local copies, waits for them, and re-layouts  2.22 us

profile of v4, /device:TPU:1, one launch (start us, length us, event | category | flops | bytes accessed | tf_op | source)
XLA Modules:
  0.0 78.8 jit_solution(1499026320278042905)
XLA Ops:
  0.6 0.0 copy-start
  0.6 0.9 %copy-done = s32[32768]{0:T(1024)S(1)} copy-done((s32[32768]{0:T(1024)S(1)}, s32[32768]{0:T(1024)}, u32[]{:S(2)}) %copy-start) | copy-done | bytes 131096
  1.5 0.0 copy-start.1
  1.5 0.7 copy-done.1
  2.2 0.0 copy-start.2
  2.2 0.7 copy-done.2
  2.9 0.0 copy-start.3
  2.9 0.0 copy-start.4
  2.9 0.0 copy-start.5
  2.9 69.1 %shard_map.111 = f32[16,512,128]{2,1,0:T(8,128)S(1)} custom-call(bf16[1,1048576]{1,0:T(2,128)(2,1)} %grad_hbm.1, s32[16,512,128]{2,1,0:T(8,128)} %bitcast.5, s32[256,128]{1,0:T(8,128)S(1)} %bitcast.4, s32[16]{0:T(128)S(1)} %copy-done.1, f32[16]{0:T(128)S(1)} %copy-done.2), custom_call_target="tpu_custom_call" | custom-call | flops 2147483648 | bytes 12582912 | tf_op jit(solution)/shard_map/pallas_call | solution.py:529
  72.0 0.0 copy-done.3
  72.0 0.0 copy-done.4
  72.0 0.0 copy-done.5
  72.0 6.8 %multiply_subtract_fusion = (f32[1048576]{0:T(1024)}, f32[1048576]{0:T(1024)}, f32[1048576]{0:T(1024)}, f32[1048576]{0:T(1024)}) fusion(f32[1048576]{0:T(1024)S(1)} %copy-done.3, f32[1048576]{0:T(1024)S(1)} %bitcast.3, f32[1048576]{0:T(1024)S(1)} %copy-done.4, f32[1048576]{0:T(1024)S(1)} %copy-done.5), kind=kLoop, calls=%fused_computation.2 | loop fusion | flops 13631488 | bytes 33554432 | tf_op jit(solution)/shard_map/sub | solution.py:581
Async XLA Ops:
  0.6 0.9 %copy-start = (s32[32768]{0:T(1024)S(1)}, s32[32768]{0:T(1024)}, u32[]{:S(2)}) copy-start(s32[32768]{0:T(1024)} %param.10) | copy-start | bytes 393220
  1.5 0.7 copy-start.1
  2.2 0.7 copy-start.2
  2.9 69.2 %copy-start.3 = (f32[1048576]{0:T(1024)S(1)}, f32[1048576]{0:T(1024)}, u32[]{:S(2)}) copy-start(f32[1048576]{0:T(1024)} %param.13) | copy-start | bytes 12582916
  2.9 69.2 %copy-start.4 = (f32[1048576]{0:T(1024)S(1)}, f32[1048576]{0:T(1024)}, u32[]{:S(2)}) copy-start(f32[1048576]{0:T(1024)} %param.14) | copy-start | bytes 12582916
  2.9 69.2 %copy-start.5 = (f32[1048576]{0:T(1024)S(1)}, f32[1048576]{0:T(1024)}, u32[]{:S(2)}) copy-start(f32[1048576]{0:T(1024)} %param.15) | copy-start | bytes 12582916

commit v5 on v4

--- a/solution.py
+++ b/solution.py
@@ -90,10 +90,10 @@
 )
 PEAK_FIRST_SLOT = (0, 7, 10)
 PEAK_COPIES = 13
-COPIES = 3 * PEAK_COPIES + 1 + PARTS * (2 + 6 + 15) + 3 * (15 + 4 * 10)
-
-
-LANDING = {"tl": 0, "th": 8, "fa": 16, "fb": 32, "plane": 48}
+COPIES = 3 * PEAK_COPIES + 1 + PARTS * (2 + 3 + 15) + 3 * (15 + 3 * 10 + 7)
+
+
+LANDING = {"ring": 0, "plane": 48}
 LANDING_UNITS = 64
 
 
@@ -136,15 +136,16 @@
     ]
     small_loads[0].start()
     span = CHUNK * LANES
-    loads = [[] for _ in WAVES]
-    for wave, parts in enumerate(WAVES):
-        for i, part in enumerate(parts):
-            for j, half in enumerate((theirs, mine)):
-                at = pl.ds(pl.multiple_of((half + part) * span, span), span)
-                loads[wave].append(
-                    pltpu.make_async_copy(grad_hbm.at[:, at], grad_v.at[:, at], grad_sems.at[part * 2 + j])
-                )
-                loads[wave][-1].start()
+
+    def grad_load(part, h):
+        chunk = (1 - core + h * (2 * core - 1)) * PARTS + part
+        at = pl.ds(pl.multiple_of(chunk * span, span), span)
+        return pltpu.make_async_copy(grad_hbm.at[:, at], grad_v.at[:, at], grad_sems.at[part, h])
+
+    for parts in WAVES:
+        for h in range(2):
+            for part in parts:
+                grad_load(part, h).start()
     for load in small_loads[1:3]:
         load.start()
 
@@ -182,14 +183,13 @@
             peaks[wave][pl.ds(half_core * 8 + (2 * i + j), 1), :] = top[:, j * LANES : (j + 1) * LANES]
 
     def rotate(wave):
-        for load in loads[wave]:
-            load.wait()
         parts = WAVES[wave]
 
         def body(h, carry):
             half_core = (1 - core) + h * (2 * core - 1)
             for i in range(len(parts) + 1):
                 if i < len(parts):
+                    grad_load(parts[i], h).wait()
                     sign_chunk(half_core * PARTS + parts[i], i % 2)
                 if i >= 1:
                     rotate_chunk(wave, half_core, i - 1, half_core * PARTS + parts[i - 1], (i - 1) % 2)
@@ -326,40 +326,17 @@
     def quarters(order):
         return [lax.rem(here.at[order[0]] + d, RING) * QUARTER for d in range(RING)]
 
-    def scatter_first(part):
+    def scatter_ring(part):
         order = order_of(part)
         at = quarters(order)
-        right, left = here.near((order[0], 1)), here.near((order[0], 3))
-
-        def move(start, name, skip, to):
-            return copies.start(
-                codes.at[part, rows_of(start, 8)], landing.at[part, rows_of(LANDING[name] + skip, 8)], to
+        ring[part] = [
+            copies.start(
+                codes.at[part, rows_of(at[d], QUARTER)],
+                landing.at[part, rows_of(LANDING["ring"] + (d - 1) * QUARTER, QUARTER)],
+                here.near((order[0], d)),
             )
-
-        ring[part] = [
-            move(at[2], "tl", 0, right),
-            move(at[2] + 8, "th", 0, left),
-            move(at[1] + 8, "fa", 8, right),
-            move(at[3], "fb", 0, left),
+            for d in (2, 1, 3)
         ]
-
-    def scatter_second(part):
-        order = order_of(part)
-        at = quarters(order)
-        right, left = here.near((order[0], 1)), here.near((order[0], 3))
-        waits = ring[part]
-        waits[0].wait_recv()
-        add_into(codes, part, at[1], landing, [LANDING["tl"]], 8)
-        waits.append(
-            copies.start(codes.at[part, rows_of(at[1], 8)], landing.at[part, rows_of(LANDING["fa"], 8)], right)
-        )
-        waits[1].wait_recv()
-        add_into(codes, part, at[3] + 8, landing, [LANDING["th"]], 8)
-        waits.append(
-            copies.start(
-                codes.at[part, rows_of(at[3] + 8, 8)], landing.at[part, rows_of(LANDING["fb"] + 8, 8)], left
-            )
-        )
 
     plane = {}
 
@@ -369,11 +346,10 @@
 
     def scatter_plane(part):
         order = order_of(part)
-        for copy in ring[part][2:]:
+        for copy in ring[part]:
             copy.wait_recv()
-        add_into(
-            codes, part, here.at[order[0]] * QUARTER, landing, [LANDING["fa"], LANDING["fb"]], QUARTER
-        )
+        firsts = [LANDING["ring"] + d * QUARTER for d in range(RING - 1)]
+        add_into(codes, part, here.at[order[0]] * QUARTER, landing, firsts, QUARTER)
         plane[part] = [
             copies.start(
                 codes.at[part, rows_of(piece_at(order, i, j), 1)],
@@ -415,15 +391,10 @@
         spread(wave)
         quantize(wave, gap_table, point_table)
         for part in WAVES[wave]:
-            scatter_first(part)
-    for part in WAVES[0] + WAVES[1]:
-        scatter_second(part)
-    for part in WAVES[0]:
-        scatter_plane(part)
-    for part in WAVES[2]:
-        scatter_second(part)
-    for part in WAVES[1] + WAVES[2]:
-        scatter_plane(part)
+            scatter_ring(part)
+    for parts in WAVES:
+        for part in parts:
+            scatter_plane(part)
     for part in range(PARTS):
         scatter_last(part)
 
@@ -475,17 +446,29 @@
         for copy in arrive[turn, i]:
             copy.wait_recv()
         at, right, left = group_of(turn, i)
-        gather[turn, i] = [
-            send(turn, at[0], 2, right),
-            send(turn, at[0] + 2, 2, left),
-            send(turn, at[0] + 2, 2, right),
-            send(turn, at[0], 2, left),
-        ]
+        if i == GROUPS[-1]:
+            gather[turn, i] = [
+                send(turn, at[0], RING, here.near((ORDERS[turn][0], 2))),
+                send(turn, at[0], RING, right),
+                send(turn, at[0], RING, left),
+            ]
+        else:
+            gather[turn, i] = [
+                send(turn, at[0], 2, right),
+                send(turn, at[0] + 2, 2, left),
+                send(turn, at[0] + 2, 2, right),
+                send(turn, at[0], 2, left),
+            ]
         last.append(send(turn, at[0], RING, sibling))
 
     def gather_second(turn, i):
         at, right, left = group_of(turn, i)
         waits = gather[turn, i]
+        if i == GROUPS[-1]:
+            for copy, d in ((waits[1], 3), (waits[2], 1), (waits[0], 2)):
+                copy.wait_recv()
+                last.append(send(turn, at[d], RING, sibling))
+            return
         waits[0].wait_recv()
         waits.append(send(turn, at[3], 2, right))
         waits[1].wait_recv()
@@ -504,16 +487,10 @@
     for i in GROUPS:
         for turn in range(3):
             gather_plane(turn, i)
-    for step in range(len(GROUPS) + 2):
-        if step < len(GROUPS):
+    for step in (gather_first, gather_second, gather_last):
+        for i in GROUPS if step is not gather_last else GROUPS[:-1]:
             for turn in range(3):
-                gather_first(turn, GROUPS[step])
-        if 0 <= step - 1 < len(GROUPS):
-            for turn in range(3):
-                gather_second(turn, GROUPS[step - 1])
-        if step >= 2:
-            for turn in range(3):
-                gather_last(turn, GROUPS[step - 2])
+                step(turn, i)
     for copy in last:
         copy.wait_recv()
     for copy in copies.late:
@@ -555,7 +532,7 @@
             pltpu.VMEM((PARTS * UNIT, LANES), jnp.float32),
             pltpu.SemaphoreType.DMA((COPIES,)),
             pltpu.SemaphoreType.DMA((COPIES,)),
-            pltpu.SemaphoreType.DMA((chunks,)),
+            pltpu.SemaphoreType.DMA((PARTS, 2)),
             pltpu.SemaphoreType.DMA((4,)),
         ],
         compiler_params=pltpu.CompilerParams(

time: 78.9 us -> 71.3 us (0.904)
  Pallas kernels: 69.1 us -> 61.5 us
    pallas_call x1, Pallas kernels: 69.1 us -> 61.5 us  [mean_gradient(): pl.pallas_call(reduce_kernel, out_shape=jax.ShapeDtypeStruct((chunks, CHU...]
where the time goes in v5:
time: 71.3 us; the launch traced here: 71.1 us
  Pallas kernels  61.5 us (86%)
  other arithmetic  6.75 us (9%)
  local copies, waits for them, and re-layouts  2.22 us (3%)
    pallas_call x1, Pallas kernels, mean_gradient(): pl.pallas_call(reduce_kernel, out_shape=jax.ShapeDtypeStruct((chunks, CHU...  61.5 us
    sub x1, other arithmetic, body(): new_params = params - step_rate * update  6.75 us
    unnamed x12, local copies, waits for them, and re-layouts  2.22 us

profile of v5, /device:TPU:1, one launch (start us, length us, event | category | flops | bytes accessed | tf_op | source)
XLA Modules:
  0.0 71.1 jit_solution(12263029897921399948)
XLA Ops:
  0.6 0.0 copy-start
  0.6 0.9 %copy-done = s32[32768]{0:T(1024)S(1)} copy-done((s32[32768]{0:T(1024)S(1)}, s32[32768]{0:T(1024)}, u32[]{:S(2)}) %copy-start) | copy-done | bytes 131096
  1.5 0.0 copy-start.1
  1.5 0.7 copy-done.1
  2.2 0.0 copy-start.2
  2.2 0.7 copy-done.2
  2.9 0.0 copy-start.3
  2.9 0.0 copy-start.4
  2.9 0.0 copy-start.5
  2.9 61.5 %shard_map.111 = f32[16,512,128]{2,1,0:T(8,128)S(1)} custom-call(bf16[1,1048576]{1,0:T(2,128)(2,1)} %grad_hbm.1, s32[16,512,128]{2,1,0:T(8,128)} %bitcast.5, s32[256,128]{1,0:T(8,128)S(1)} %bitcast.4, s32[16]{0:T(128)S(1)} %copy-done.1, f32[16]{0:T(128)S(1)} %copy-done.2), custom_call_target="tpu_custom_call" | custom-call | flops 2147483648 | bytes 12582912 | tf_op jit(solution)/shard_map/pallas_call | solution.py:506
  64.3 0.0 copy-done.3
  64.3 0.0 copy-done.4
  64.4 0.0 copy-done.5
  64.4 6.8 %multiply_subtract_fusion = (f32[1048576]{0:T(1024)}, f32[1048576]{0:T(1024)}, f32[1048576]{0:T(1024)}, f32[1048576]{0:T(1024)}) fusion(f32[1048576]{0:T(1024)S(1)} %copy-done.3, f32[1048576]{0:T(1024)S(1)} %bitcast.3, f32[1048576]{0:T(1024)S(1)} %copy-done.4, f32[1048576]{0:T(1024)S(1)} %copy-done.5), kind=kLoop, calls=%fused_computation.2 | loop fusion | flops 13631488 | bytes 33554432 | tf_op jit(solution)/shard_map/sub | solution.py:558
Async XLA Ops:
  0.6 0.9 %copy-start = (s32[32768]{0:T(1024)S(1)}, s32[32768]{0:T(1024)}, u32[]{:S(2)}) copy-start(s32[32768]{0:T(1024)} %param.10) | copy-start | bytes 393220
  1.5 0.7 copy-start.1
  2.2 0.7 copy-start.2
  2.9 61.5 %copy-start.3 = (f32[1048576]{0:T(1024)S(1)}, f32[1048576]{0:T(1024)}, u32[]{:S(2)}) copy-start(f32[1048576]{0:T(1024)} %param.13) | copy-start | bytes 12582916
  2.9 61.5 %copy-start.4 = (f32[1048576]{0:T(1024)S(1)}, f32[1048576]{0:T(1024)}, u32[]{:S(2)}) copy-start(f32[1048576]{0:T(1024)} %param.14) | copy-start | bytes 12582916
  2.9 61.5 %copy-start.5 = (f32[1048576]{0:T(1024)S(1)}, f32[1048576]{0:T(1024)}, u32[]{:S(2)}) copy-start(f32[1048576]{0:T(1024)} %param.15) | copy-start | bytes 12582916

commit v6 on v5

--- a/solution.py
+++ b/solution.py
@@ -85,12 +85,11 @@
 
 PEAK_ROUNDS = (
     tuple((("x", i), ("core", j)) for i in (2, 1, 3, 0) for j in (1, 0) if i + j),
-    tuple((("y", i),) for i in (2, 1, 3)),
-    tuple((("z", i),) for i in (2, 1, 3)),
+    tuple((("y", i), ("z", j)) for i, j in PLANE),
 )
-PEAK_FIRST_SLOT = (0, 7, 10)
-PEAK_COPIES = 13
-COPIES = 3 * PEAK_COPIES + 1 + PARTS * (2 + 3 + 15) + 3 * (15 + 3 * 10 + 7)
+PEAK_FIRST_SLOT = (0, 7)
+PEAK_COPIES = 22
+COPIES = 3 * PEAK_COPIES + 1 + PARTS * (2 + 3 + 15) + 3 * (15 + 4 * 7)
 
 
 LANDING = {"ring": 0, "plane": 48}
@@ -119,7 +118,7 @@
     mine, theirs = core * PARTS, (1 - core) * PARTS
 
     barrier = pltpu.get_barrier_semaphore()
-    partners = [here.near(*moves) for moves in PEAK_ROUNDS[0] + PEAK_ROUNDS[1] + PEAK_ROUNDS[2]]
+    partners = [here.near(*moves) for moves in PEAK_ROUNDS[0] + PEAK_ROUNDS[1]]
     for partner in partners:
         pl.semaphore_signal(barrier, inc=1, device_id=partner, device_id_type=MESH)
 
@@ -381,13 +380,12 @@
     for load in small_loads[1:]:
         load.wait()
     gap_table, point_table = tables()
-    for turn in (0, 1):
-        for wave in range(3):
-            peak_take(wave, turn)
-            peak_send(wave, turn + 1)
+    for wave in range(3):
+        peak_take(wave, 0)
+        peak_send(wave, 1)
     near_dither_copy.wait_recv()
     for wave in range(3):
-        peak_take(wave, 2)
+        peak_take(wave, 1)
         spread(wave)
         quantize(wave, gap_table, point_table)
         for part in WAVES[wave]:
@@ -439,56 +437,26 @@
     def group_of(turn, i):
         order = ORDERS[turn]
         skip = lax.rem(here.at[order[1]] + i, RING) * RING
-        starts = [start + skip for start in quarters(order)]
-        return starts, here.near((order[0], 1)), here.near((order[0], 3))
+        return [start + skip for start in quarters(order)]
 
     def gather_first(turn, i):
         for copy in arrive[turn, i]:
             copy.wait_recv()
-        at, right, left = group_of(turn, i)
-        if i == GROUPS[-1]:
-            gather[turn, i] = [
-                send(turn, at[0], RING, here.near((ORDERS[turn][0], 2))),
-                send(turn, at[0], RING, right),
-                send(turn, at[0], RING, left),
-            ]
-        else:
-            gather[turn, i] = [
-                send(turn, at[0], 2, right),
-                send(turn, at[0] + 2, 2, left),
-                send(turn, at[0] + 2, 2, right),
-                send(turn, at[0], 2, left),
-            ]
+        at = group_of(turn, i)
+        gather[turn, i] = [(d, send(turn, at[0], RING, here.near((ORDERS[turn][0], d)))) for d in (2, 1, 3)]
         last.append(send(turn, at[0], RING, sibling))
 
     def gather_second(turn, i):
-        at, right, left = group_of(turn, i)
-        waits = gather[turn, i]
-        if i == GROUPS[-1]:
-            for copy, d in ((waits[1], 3), (waits[2], 1), (waits[0], 2)):
-                copy.wait_recv()
-                last.append(send(turn, at[d], RING, sibling))
-            return
-        waits[0].wait_recv()
-        waits.append(send(turn, at[3], 2, right))
-        waits[1].wait_recv()
-        waits.append(send(turn, at[1] + 2, 2, left))
-        waits[2].wait_recv()
-        waits[3].wait_recv()
-        last.append(send(turn, at[3], RING, sibling))
-        last.append(send(turn, at[1], RING, sibling))
-
-    def gather_last(turn, i):
-        at, _, _ = group_of(turn, i)
-        for copy in gather[turn, i][4:]:
+        at = group_of(turn, i)
+        for d, copy in gather[turn, i][1:] + gather[turn, i][:1]:
             copy.wait_recv()
-        last.append(send(turn, at[2], RING, sibling))
+            last.append(send(turn, at[RING - d], RING, sibling))
 
     for i in GROUPS:
         for turn in range(3):
             gather_plane(turn, i)
-    for step in (gather_first, gather_second, gather_last):
-        for i in GROUPS if step is not gather_last else GROUPS[:-1]:
+    for step in (gather_first, gather_second):
+        for i in GROUPS:
             for turn in range(3):
                 step(turn, i)
     for copy in last:

time: 71.3 us -> 69.1 us (0.969)
  Pallas kernels: 61.5 us -> 59.3 us
    pallas_call x1, Pallas kernels: 61.5 us -> 59.3 us  [mean_gradient(): pl.pallas_call(reduce_kernel, out_shape=jax.ShapeDtypeStruct((chunks, CHU...]
where the time goes in v6:
time: 69.1 us; the launch traced here: 69 us
  Pallas kernels  59.3 us (86%)
  other arithmetic  6.75 us (10%)
  local copies, waits for them, and re-layouts  2.22 us (3%)
    pallas_call x1, Pallas kernels, mean_gradient(): pl.pallas_call(reduce_kernel, out_shape=jax.ShapeDtypeStruct((chunks, CHU...  59.3 us
    sub x1, other arithmetic, body(): new_params = params - step_rate * update  6.75 us
    unnamed x12, local copies, waits for them, and re-layouts  2.22 us

profile of v6, /device:TPU:1, one launch (start us, length us, event | category | flops | bytes accessed | tf_op | source)
XLA Modules:
  0.0 69.0 jit_solution(14338615793525813337)
XLA Ops:
  0.6 0.0 copy-start
  0.6 0.9 %copy-done = s32[32768]{0:T(1024)S(1)} copy-done((s32[32768]{0:T(1024)S(1)}, s32[32768]{0:T(1024)}, u32[]{:S(2)}) %copy-start) | copy-done | bytes 131096
  1.5 0.0 copy-start.1
  1.5 0.7 copy-done.1
  2.2 0.0 copy-start.2
  2.2 0.7 copy-done.2
  2.9 0.0 copy-start.3
  2.9 0.0 copy-start.4
  2.9 0.0 copy-start.5
  2.9 59.3 %shard_map.111 = f32[16,512,128]{2,1,0:T(8,128)S(1)} custom-call(bf16[1,1048576]{1,0:T(2,128)(2,1)} %grad_hbm.1, s32[16,512,128]{2,1,0:T(8,128)} %bitcast.5, s32[256,128]{1,0:T(8,128)S(1)} %bitcast.4, s32[16]{0:T(128)S(1)} %copy-done.1, f32[16]{0:T(128)S(1)} %copy-done.2), custom_call_target="tpu_custom_call" | custom-call | flops 2147483648 | bytes 12582912 | tf_op jit(solution)/shard_map/pallas_call | solution.py:474
  62.2 0.0 copy-done.3
  62.2 0.0 copy-done.4
  62.2 0.0 copy-done.5
  62.2 6.8 %multiply_subtract_fusion = (f32[1048576]{0:T(1024)}, f32[1048576]{0:T(1024)}, f32[1048576]{0:T(1024)}, f32[1048576]{0:T(1024)}) fusion(f32[1048576]{0:T(1024)S(1)} %copy-done.3, f32[1048576]{0:T(1024)S(1)} %bitcast.3, f32[1048576]{0:T(1024)S(1)} %copy-done.4, f32[1048576]{0:T(1024)S(1)} %copy-done.5), kind=kLoop, calls=%fused_computation.2 | loop fusion | flops 13631488 | bytes 33554432 | tf_op jit(solution)/shard_map/sub | solution.py:526
Async XLA Ops:
  0.6 0.9 %copy-start = (s32[32768]{0:T(1024)S(1)}, s32[32768]{0:T(1024)}, u32[]{:S(2)}) copy-start(s32[32768]{0:T(1024)} %param.10) | copy-start | bytes 393220
  1.5 0.7 copy-start.1
  2.2 0.7 copy-start.2
  2.9 59.3 %copy-start.3 = (f32[1048576]{0:T(1024)S(1)}, f32[1048576]{0:T(1024)}, u32[]{:S(2)}) copy-start(f32[1048576]{0:T(1024)} %param.13) | copy-start | bytes 12582916
  2.9 59.3 %copy-start.4 = (f32[1048576]{0:T(1024)S(1)}, f32[1048576]{0:T(1024)}, u32[]{:S(2)}) copy-start(f32[1048576]{0:T(1024)} %param.14) | copy-start | bytes 12582916
  2.9 59.4 %copy-start.5 = (f32[1048576]{0:T(1024)S(1)}, f32[1048576]{0:T(1024)}, u32[]{:S(2)}) copy-start(f32[1048576]{0:T(1024)} %param.15) | copy-start | bytes 12582916

commit v7 on v6

--- a/solution.py
+++ b/solution.py
@@ -108,7 +108,7 @@
     grad_hbm, dither_hbm, words_hbm, values_hbm, points_hbm, out,
     grad_v, dither_v, words, level_values, level_points, signed, coef_even, coef_odd, codes,
     peak_a, peak_b, peak_c, peak_in, high_all, low_all, ratio_all,
-    near_even, near_odd, near_dither, landing, owned, send_sems, recv_sems, grad_sems, load_sems,
+    near_even, near_odd, near_dither, landing, owned, send_sems, recv_sems, grad_sems, load_sems, plane_ready,
 ):
     here = Place()
     core = here.at["core"]
@@ -118,7 +118,8 @@
     mine, theirs = core * PARTS, (1 - core) * PARTS
 
     barrier = pltpu.get_barrier_semaphore()
-    partners = [here.near(*moves) for moves in PEAK_ROUNDS[0] + PEAK_ROUNDS[1]]
+    axes = tuple(((axis, i),) for axis in ("y", "z") for i in (2, 1, 3))
+    partners = [here.near(*moves) for moves in PEAK_ROUNDS[0] + axes]
     for partner in partners:
         pl.semaphore_signal(barrier, inc=1, device_id=partner, device_id_type=MESH)
 
@@ -184,17 +185,16 @@
     def rotate(wave):
         parts = WAVES[wave]
 
-        def body(h, carry):
-            half_core = (1 - core) + h * (2 * core - 1)
-            for i in range(len(parts) + 1):
-                if i < len(parts):
-                    grad_load(parts[i], h).wait()
-                    sign_chunk(half_core * PARTS + parts[i], i % 2)
-                if i >= 1:
-                    rotate_chunk(wave, half_core, i - 1, half_core * PARTS + parts[i - 1], (i - 1) % 2)
-            return carry
-
-        lax.fori_loop(0, 2, body, 0)
+        steps = [(h, i) for h in range(2) for i in range(len(parts))]
+        half_core = (1 - core, core)
+        for t in range(len(steps) + 1):
+            if t < len(steps):
+                h, i = steps[t]
+                grad_load(parts[i], h).wait()
+                sign_chunk(half_core[h] * PARTS + parts[i], t % 2)
+            if t >= 1:
+                h, i = steps[t - 1]
+                rotate_chunk(wave, half_core[h], i, half_core[h] * PARTS + parts[i], (t - 1) % 2)
 
     near_copies = {}
 
@@ -279,7 +279,13 @@
                 else:
                     value = (near_even, near_odd)[p][part, at, :]
                 place = jnp.minimum((value * ratio_all[part, at, :] + 32.0).astype(jnp.int32), 63)
-                held[m, p, own] = (value, place, take(gap_table, place))
+                if p:
+                    packed = take(gap_table, place)
+                else:
+                    packed = jnp.full((UNIT, LANES), gaps[0], jnp.float32)
+                    for j in range(1, 15):
+                        packed = jnp.where(place >= level_cells[j], gaps[j], packed)
+                held[m, p, own] = (value, place, packed)
 
         def round_cells(batch):
             for m, p, own in batch:
@@ -367,6 +373,8 @@
     small_loads[0].wait()
     rotate(0)
     pl.semaphore_wait(barrier, len(partners))
+    for moves in axes[:3]:
+        pl.semaphore_signal(plane_ready, inc=1, device_id=here.near(*moves), device_id_type=MESH)
     peak_send(0, 0)
     small_loads[3].start()
     near_dither_copy = copies.start(dither_hbm.at[pl.ds(theirs, PARTS)], near_dither, sibling)
@@ -380,6 +388,12 @@
     for load in small_loads[1:]:
         load.wait()
     gap_table, point_table = tables()
+    level_cells = [level_values[j] + 32 for j in range(15)]
+    gaps = [
+        level_values[j].astype(jnp.float32) + (level_values[j + 1] - level_values[j]).astype(jnp.float32) / 64.0
+        for j in range(15)
+    ]
+    pl.semaphore_wait(plane_ready, 3)
     for wave in range(3):
         peak_take(wave, 0)
         peak_send(wave, 1)
@@ -502,6 +516,7 @@
             pltpu.SemaphoreType.DMA((COPIES,)),
             pltpu.SemaphoreType.DMA((PARTS, 2)),
             pltpu.SemaphoreType.DMA((4,)),
+            pltpu.SemaphoreType.REGULAR,
         ],
         compiler_params=pltpu.CompilerParams(
             collective_id=0, has_side_effects=True, vmem_limit_bytes=47 * 2**20

time: 69.1 us -> 68.3 us (0.988)
  Pallas kernels: 59.3 us -> 58.5 us
    pallas_call x1, Pallas kernels: 59.3 us -> 58.5 us  [mean_gradient(): pl.pallas_call(reduce_kernel, out_shape=jax.ShapeDtypeStruct((chunks, CHU...]
where the time goes in v7:
time: 68.3 us; the launch traced here: 68.2 us
  Pallas kernels  58.5 us (86%)
  other arithmetic  6.75 us (10%)
  local copies, waits for them, and re-layouts  2.22 us (3%)
    pallas_call x1, Pallas kernels, mean_gradient(): pl.pallas_call(reduce_kernel, out_shape=jax.ShapeDtypeStruct((chunks, CHU...  58.5 us
    sub x1, other arithmetic, body(): new_params = params - step_rate * update  6.75 us
    unnamed x12, local copies, waits for them, and re-layouts  2.22 us

profile of v7, /device:TPU:1, one launch (start us, length us, event | category | flops | bytes accessed | tf_op | source)
XLA Modules:
  0.0 68.2 jit_solution(535921834804780734)
XLA Ops:
  0.6 0.0 copy-start
  0.6 0.9 %copy-done = s32[32768]{0:T(1024)S(1)} copy-done((s32[32768]{0:T(1024)S(1)}, s32[32768]{0:T(1024)}, u32[]{:S(2)}) %copy-start) | copy-done | bytes 131096
  1.5 0.0 copy-start.1
  1.5 0.7 copy-done.1
  2.2 0.0 copy-start.2
  2.2 0.7 copy-done.2
  2.9 0.0 copy-start.3
  2.9 0.0 copy-start.4
  2.9 0.0 copy-start.5
  2.9 58.5 %shard_map.111 = f32[16,512,128]{2,1,0:T(8,128)S(1)} custom-call(bf16[1,1048576]{1,0:T(2,128)(2,1)} %grad_hbm.1, s32[16,512,128]{2,1,0:T(8,128)} %bitcast.5, s32[256,128]{1,0:T(8,128)S(1)} %bitcast.4, s32[16]{0:T(128)S(1)} %copy-done.1, f32[16]{0:T(128)S(1)} %copy-done.2), custom_call_target="tpu_custom_call" | custom-call | flops 2147483648 | bytes 12582912 | tf_op jit(solution)/shard_map/pallas_call | solution.py:488
  61.4 0.0 copy-done.3
  61.4 0.0 copy-done.4
  61.4 0.0 copy-done.5
  61.4 6.8 %multiply_subtract_fusion = (f32[1048576]{0:T(1024)}, f32[1048576]{0:T(1024)}, f32[1048576]{0:T(1024)}, f32[1048576]{0:T(1024)}) fusion(f32[1048576]{0:T(1024)S(1)} %copy-done.3, f32[1048576]{0:T(1024)S(1)} %bitcast.3, f32[1048576]{0:T(1024)S(1)} %copy-done.4, f32[1048576]{0:T(1024)S(1)} %copy-done.5), kind=kLoop, calls=%fused_computation.2 | loop fusion | flops 13631488 | bytes 33554432 | tf_op jit(solution)/shard_map/sub | solution.py:541
Async XLA Ops:
  0.6 0.9 %copy-start = (s32[32768]{0:T(1024)S(1)}, s32[32768]{0:T(1024)}, u32[]{:S(2)}) copy-start(s32[32768]{0:T(1024)} %param.10) | copy-start | bytes 393220
  1.5 0.7 copy-start.1
  2.2 0.7 copy-start.2
  2.9 58.5 %copy-start.3 = (f32[1048576]{0:T(1024)S(1)}, f32[1048576]{0:T(1024)}, u32[]{:S(2)}) copy-start(f32[1048576]{0:T(1024)} %param.13) | copy-start | bytes 12582916
  2.9 58.5 %copy-start.4 = (f32[1048576]{0:T(1024)S(1)}, f32[1048576]{0:T(1024)}, u32[]{:S(2)}) copy-start(f32[1048576]{0:T(1024)} %param.14) | copy-start | bytes 12582916
  2.9 58.6 %copy-start.5 = (f32[1048576]{0:T(1024)S(1)}, f32[1048576]{0:T(1024)}, u32[]{:S(2)}) copy-start(f32[1048576]{0:T(1024)} %param.15) | copy-start | bytes 12582916
